TPU v7x, 32 devices: a whole 2x2x4 slice. The times are simulated.
32 devices in a mesh: rollout: 2 (over core), context: 4 (over z), head: 4 (over y, x).
Axes of the slice: x: 2, y: 2, z: 4, core: 2. Of those that a mesh axis runs over, the one named last changes fastest.
Arguments:
- inner_raw: bfloat16 [2048, 8192], P(('rollout', 'context', 'head')), parts along dimension 0, may hold values from -6 to 6
- pairs_raw: bfloat16 [2048, 8, 2, 128], P(('rollout', 'context', 'head')), parts along dimension 0, may hold values from -2.5 to 2.5
- gate_raw: bfloat16 [2048, 8192], P(('rollout', 'context'), 'head'), parts along dimension 0, may hold values from -6 to 6
- step_raw: bfloat16 [2048, 128], P(('rollout', 'context'), 'head'), parts along dimension 0, may hold values from -3 to 3
- step_bias: float32 [128], P('head'), may hold values from -0.5 to 0.5
- rate_log: float32 [128], P('head'), may hold values from -13.5 to -2.8, as said below
- skip_gain: float32 [128], P('head'), may hold values from 0.5 to 2
- conv_inner: float32 [5, 8192], replicated, may hold values from -2.5 to 2.5
- conv_pairs: float32 [5, 8, 2, 128], replicated, may hold values from -2.5 to 2.5
- norm_gain: float32 [8192], P('head'), may hold values from 0.5 to 1.5
Outputs:
- mixer_out: bfloat16 [2048, 8192], P(('rollout', 'context', 'head')), parts along dimension 0
There are 2 independent parts, one for each index of `rollout`. A program takes and returns all parts, laid end to end along the dimension named above; an argument that names none is the same for every part. Nothing has to cross between parts.
Inputs may be any that keep to these rules, and one draw needn't show every extreme that they name: `rate_log`: one value a head.
All inputs are finite; a program needn't handle non-finite values.
Results may differ from a plain program's by a relative error of at most 0.012.
The roundings to bfloat16 on the way count: a program that leaves them out, or rounds other values in their place, can miss the bound.
Values may be sent and summed in bfloat16 or wider, within the bound.
A program may use at most 128 MiB of HBM per device.

v0:
```python
import jax
import jax.numpy as jnp
from jax import lax
from jax.sharding import PartitionSpec as P

BLOCK = 256


def from_behind(block, axis, distance):
    devices = range(lax.axis_size(axis))
    route = [(i - distance, i) for i in devices if i - distance in devices]
    return lax.ppermute(block, axis, route)


def prefix(part, axis, combine, identity):
    place = lax.axis_index(axis)
    gathered = jax.tree.map(lambda a: lax.all_gather(a, axis), part)
    state = jax.tree.map(lambda a, e: jnp.zeros_like(a) + jnp.asarray(e, a.dtype), part, identity)

    def one(lap, state):
        return combine(
            state, jax.tree.map(lambda a: lax.dynamic_index_in_dim(a, lap, 0, False), gathered)
        )

    return lax.fori_loop(0, place, one, state)


def convolve(raw_rows, before, weight):
    tap_count = weight.shape[0] - 1
    row_count = raw_rows.shape[0]
    extended = jnp.concatenate([before, raw_rows], axis=0).astype(jnp.float32)
    summed = weight[tap_count][None, :] + weight[0][None, :] * extended[0:row_count]
    for offset in range(1, tap_count):
        summed = summed + weight[offset][None, :] * extended[offset : offset + row_count]
    return jax.nn.silu(summed).astype(jnp.bfloat16)


def block_intra(inner_conv, pairs_conv, step_size, log_cum, groups):
    block_len, head_count = step_size.shape
    per_group = head_count // groups
    head_width = inner_conv.shape[1] // head_count
    pair_view = pairs_conv.reshape(block_len, groups, 2, -1)
    scores = jnp.einsum(
        "ign,jgn->gij", pair_view[:, :, 1], pair_view[:, :, 0], preferred_element_type=jnp.float32
    )
    lower_tri = lax.broadcasted_iota(jnp.int32, (block_len, block_len), 0) >= lax.broadcasted_iota(
        jnp.int32, (block_len, block_len), 1
    )
    cum_t = log_cum.T
    log_gap = jnp.minimum(cum_t[:, :, None] - cum_t[:, None, :], 0.0)
    decay_mat = jnp.where(lower_tri[None], jnp.exp(log_gap), 0.0) * step_size.T[:, None, :]
    weights = (scores[:, None] * decay_mat.reshape(groups, per_group, block_len, block_len)).astype(
        jnp.bfloat16
    )
    inner_view = inner_conv.reshape(block_len, groups, per_group, head_width)
    intra_out = jnp.einsum(
        "gkij,jgkp->igkp", weights, inner_view, preferred_element_type=jnp.float32
    )
    return intra_out.reshape(block_len, head_count * head_width)


def block_state(inner_conv, pairs_conv, step_size, log_cum, groups):
    block_len, head_count = step_size.shape
    per_group = head_count // groups
    head_width = inner_conv.shape[1] // head_count
    tail_w = jnp.exp(log_cum[-1][None, :] - log_cum) * step_size
    weighted = (
        inner_conv.reshape(block_len, head_count, head_width).astype(jnp.float32)
        * tail_w[:, :, None]
    ).astype(jnp.bfloat16)
    weighted = weighted.reshape(block_len, groups, per_group, head_width)
    bmat = pairs_conv.reshape(block_len, groups, 2, -1)[:, :, 0]
    local_state = jnp.einsum("jgn,jgkp->gknp", bmat, weighted, preferred_element_type=jnp.float32)
    return (local_state.reshape(head_count, -1, head_width), jnp.exp(log_cum[-1]))


def finish(
    inner_conv, pairs_conv, gate_rows, intra_out, carry_state, log_cum, skip_gain, norm_gain, groups
):
    block_len, head_count = log_cum.shape
    per_group = head_count // groups
    head_width = inner_conv.shape[1] // head_count
    cmat = pairs_conv.reshape(block_len, groups, 2, -1)[:, :, 1]
    held = carry_state.astype(jnp.bfloat16).reshape(groups, per_group, -1, head_width)
    carried = jnp.einsum("ign,gknp->igkp", cmat, held, preferred_element_type=jnp.float32)
    carried = carried.reshape(block_len, head_count, head_width) * jnp.exp(log_cum)[:, :, None]
    mixed = (
        intra_out
        + carried.reshape(block_len, -1)
        + jnp.repeat(skip_gain, head_width)[None, :] * inner_conv.astype(jnp.float32)
    )
    gated_out = mixed * jax.nn.silu(gate_rows.astype(jnp.float32))
    grouped = gated_out.reshape(block_len, groups, -1)
    inv_rms = lax.rsqrt(jnp.mean(grouped * grouped, axis=2, keepdims=True) + 1e-05)
    return ((grouped * inv_rms).reshape(block_len, -1) * norm_gain[None, :]).astype(jnp.bfloat16)


def chain_combine(earlier, later):
    return (earlier[0] * later[0], later[0][:, None, None] * earlier[1] + later[1])


def absorb(running, element):
    local_state, block_decay = element
    return (block_decay[:, None, None] * running + local_state, None)


def on_device(
    inner_raw,
    pairs_raw,
    gate_raw,
    step_raw,
    step_bias,
    rate_log,
    skip_gain,
    conv_inner,
    conv_pairs,
    norm_gain,
):
    shards = lax.axis_size("head")
    row_count = inner_raw.shape[0]
    tap_count = conv_inner.shape[0] - 1
    inner_full = inner_raw.shape[1]
    pairs_flat = pairs_raw.reshape(row_count, -1)
    conv_flat = conv_pairs.reshape(tap_count + 1, -1)
    width_local = gate_raw.shape[1]
    head_local = step_raw.shape[1]
    groups_local = pairs_raw.shape[1] // shards
    last_rows = jnp.concatenate(
        [inner_raw[row_count - tap_count :], pairs_flat[row_count - tap_count :]], axis=1
    )
    before = from_behind(last_rows, ("context", "head"), 1)
    outgoing_inner = convolve(inner_raw, before[:, :inner_full], conv_inner)
    outgoing_pairs = convolve(pairs_flat, before[:, inner_full:], conv_flat)
    got_inner, got_pairs = (
        lax.all_to_all(outgoing_inner, "head", split_axis=1, concat_axis=0, tiled=True),
        lax.all_to_all(outgoing_pairs, "head", split_axis=1, concat_axis=0, tiled=True),
    )
    length = got_inner.shape[0]
    block_count = length // BLOCK
    step_size = jax.nn.softplus(step_raw.astype(jnp.float32) + step_bias[None, :])
    log_steps = (-jnp.exp(rate_log)[None, :] * step_size).reshape(block_count, BLOCK, head_local)
    lower_tri = (
        lax.broadcasted_iota(jnp.int32, (BLOCK, BLOCK), 0)
        >= lax.broadcasted_iota(jnp.int32, (BLOCK, BLOCK), 1)
    ).astype(jnp.float32)
    log_cum = jnp.einsum("ij,cjh->cih", lower_tri, log_steps, precision=lax.Precision.HIGHEST)
    step_blocks = step_size.reshape(block_count, BLOCK, head_local)
    inner_blocks = got_inner.reshape(block_count, BLOCK, -1)
    pair_blocks = got_pairs.reshape(block_count, BLOCK, -1)
    gate_blocks = gate_raw.reshape(block_count, BLOCK, -1)
    inputs = (inner_blocks, pair_blocks, step_blocks, log_cum)

    def intra_part(element):
        return block_intra(element[0], element[1], element[2], element[3], groups_local)

    def state_part(element):
        return block_state(element[0], element[1], element[2], element[3], groups_local)

    def both_parts(element):
        local_state, block_decay = state_part(element)
        return (intra_part(element), local_state, block_decay)

    intra_all, states, decays = lax.map(both_parts, inputs)
    start_zero = jnp.zeros(states.shape[1:], jnp.float32)
    device_state, _ = lax.scan(absorb, start_zero, (states, decays))
    device_decay = jnp.prod(decays, axis=0)
    incoming = prefix(
        (device_decay, device_state),
        "context",
        chain_combine,
        (jnp.ones_like(device_decay), jnp.zeros_like(device_state)),
    )

    def emit(carry_state, element):
        inner_rows, pair_rows, gate_rows, intra_out, cum_rows, local_state, block_decay = element
        result = finish(
            inner_rows,
            pair_rows,
            gate_rows,
            intra_out,
            carry_state,
            cum_rows,
            skip_gain,
            norm_gain,
            groups_local,
        )
        return (block_decay[:, None, None] * carry_state + local_state, result)

    _, results = lax.scan(
        emit,
        incoming[1],
        (inner_blocks, pair_blocks, gate_blocks, intra_all, log_cum, states, decays),
    )
    head_rows = results.reshape(length, width_local)
    return lax.all_to_all(head_rows, "head", split_axis=0, concat_axis=1, tiled=True)


def solution(mesh):
    placed = (
        P(("rollout", "context", "head"), None),
        P(("rollout", "context", "head"), None, None, None),
        P(("rollout", "context"), "head"),
        P(("rollout", "context"), "head"),
        P("head"),
        P("head"),
        P("head"),
        P(),
        P(),
        P("head"),
    )
    return jax.shard_map(
        on_device,
        mesh=mesh,
        in_specs=placed,
        out_specs=P(("rollout", "context", "head"), None),
        check_vma=False,
    )
```

profile of v0, /device:TPU:26, one launch (start us, length us, event | category | flops | bytes accessed | tf_op | source)
XLA Modules:
  0.0 179.6 jit_solution(5668269810720859438)
XLA Ops:
  6.5 0.7 slice.94
  7.3 0.9 slice.93
  8.3 3.4 %collective-permute-start = (bf16[4,10240]{1,0:T(4,128)(2,1)S(1)}, bf16[4,10240]{1,0:T(4,128)(2,1)S(1)}, u32[]{:S(2)}, u32[]{:S(2)}) collective-permute-start(bf16[4,10240]{1,0:T(4,128)(2,1)S(1)} %pad_maximum_fusion), channel_id=1, source_target_pairs={{0,1},{1,2},{2,3},{3,4},{4,5},{5,6},{6,7},{7,8},{8,9},{9,10},{10,1... | collective-permute-start | bytes 245768 | tf_op jit(solution)/shard_map/ppermute | solution.py:12
  11.7 0.7 exponential_negate_fusion
  12.3 0.8 copy.88
  13.2 1.8 fusion.49
  15.0 1.0 fusion.38
  16.0 0.8 fusion.50
  16.8 1.1 reshape.198
  17.9 0.1 copy.91
  18.0 0.0 copy-start.5
  18.0 0.1 maximum_convert_fusion.1
  18.1 0.3 multiply_convert_fusion.3
  18.5 0.7 copy.132
  19.2 3.9 %all-to-all-start.1 = ((bf16[64,4,512]{2,0,1:T(8,128)(2,1)}), bf16[64,4,512]{2,0,1:T(8,128)(2,1)S(1)}, u32[]{:S(2)}, u32[]{:S(2)}) async-start(bf16[64,4,512]{2,0,1:T(8,128)(2,1)} %bitcast.111), calls=%async_computation.1 | async-start | bytes 524288 | tf_op jit(solution)/shard_map/all_to_all | solution.py:136
  23.1 0.3 maximum_convert_fusion
  23.4 1.3 multiply_convert_fusion.2
  24.8 0.0 copy-start.16
  24.8 1.0 copy.131
  25.8 1.9 %all-to-all-done.1 = bf16[64,4,512]{2,0,1:T(8,128)(2,1)S(1)} async-done(((bf16[64,4,512]{2,0,1:T(8,128)(2,1)}), bf16[64,4,512]{2,0,1:T(8,128)(2,1)S(1)}, u32[]{:S(2)}, u32[]{:S(2)}) %all-to-all-start.1) | async-done | bytes 262176 | tf_op jit(solution)/shard_map/all_to_all | solution.py:136
  27.7 4.2 %all-to-all-start = ((bf16[64,4,2048]{2,0,1:T(8,128)(2,1)}), bf16[64,4,2048]{2,0,1:T(8,128)(2,1)S(1)}, u32[]{:S(2)}, u32[]{:S(2)}) async-start(bf16[64,4,2048]{2,0,1:T(8,128)(2,1)} %bitcast.110), calls=%async_computation | async-start | bytes 2097152 | tf_op jit(solution)/shard_map/all_to_all | solution.py:135
  32.0 0.8 bitcast_exponential_fusion
  32.8 0.7 copy.93
  33.5 0.1 reshape.199
  33.6 1.1 fusion.48
  34.6 9.2 %all-to-all-done = bf16[64,4,2048]{2,0,1:T(8,128)(2,1)S(1)} async-done(((bf16[64,4,2048]{2,0,1:T(8,128)(2,1)}), bf16[64,4,2048]{2,0,1:T(8,128)(2,1)S(1)}, u32[]{:S(2)}, u32[]{:S(2)}) %all-to-all-start) | async-done | bytes 1048608 | tf_op jit(solution)/shard_map/all_to_all | solution.py:135
  43.9 2.2 %reshape.197 = bf16[256,2,16,64]{3,2,1,0:T(8,128)(2,1)S(1)} reshape(bf16[4,64,2048]{2,1,0:T(8,128)(2,1)S(1)} %bitcast.116) | data formatting | bytes 2097152 | tf_op jit(solution)/shard_map/while/body/eval_jaxpr/reshape | solution.py:55
  46.0 2.5 %copy.90 = bf16[256,2,16,64]{0,3,2,1:T(8,128)(2,1)} copy(bf16[256,2,16,64]{3,2,1,0:T(8,128)(2,1)S(1)} %reshape.197) | data formatting | bytes 2097152 | tf_op jit(solution)/shard_map/while/body/eval_jaxpr/reshape | solution.py:55
  48.5 1.7 fusion.23
  50.3 1.2 bitcast_add_fusion.1
  51.4 0.0 all-gather.3.cloned.1.call-update
  51.5 0.6 broadcast_in_dim.64
  52.1 0.1 broadcast_in_dim.63
  52.1 0.1 mul.314
  52.3 0.7 copy.99
  52.9 0.1 copy.96
  53.0 0.7 copy.89
  53.7 1.3 copy.98
  55.0 7.3 %all-gather = f32[4,1,32]{2,1,0:T(1,128)S(1)} all-gather(f32[1,1,32]{2,1,0:T(1,128)S(1)} %get-tuple-element.157), channel_id=2, replica_groups=mesh['rollout'=2,'context'=4,'head'=4] {'context'}, dimensions={0}, use_global_device_ids=true | all-gather | bytes 640 | tf_op jit(solution)/shard_map/all_gather | solution.py:17
  62.3 1.0 fusion.35
  63.3 0.3 bitcast_convert_fusion
  63.6 0.0 copy-start.1
  63.7 1.9 %copy.97 = f32[256,2048]{0,1:T(8,128)} copy(f32[256,2048]{1,0:T(8,128)S(1)} %bitcast_convert_fusion) | data formatting | bytes 4194304 | tf_op jit(solution)/shard_map/while/body/eval_jaxpr/convert_element_type | solution.py:90
  65.5 5.3 %fusion = f32[2,16,64,256]{3,2,1,0:T(8,128)} fusion(bf16[256,2,16,64]{0,3,2,1:T(8,128)(2,1)S(1)} %copy-done.1, f32[2,16,256]{2,1,0:T(8,128)S(1)} %bitcast.138, f32[2,16,256]{2,1,0:T(8,128)S(1)} %bitcast.136, f32[2,256,256]{2,1,0:T(8,128)} %fusion.35, pred[256,256]{1,0:T(8,128)(4,1)S(1)} %iota_compare_fusion), kind=kOutput, calls=%fused_computation.4 | convolution fusion | flops 281018368 | bytes 3801088 | tf_op jit(solution)/shard_map/while/body/eval_jaxpr/gkij,jgkp->igkp/dot_general | solution.py:56
  70.9 59.1 %all-gather.3.cloned.1.call-done = f32[4,32,128,64]{2,3,1,0:T(8,128)} async-done(((f32[1,32,128,64]{2,3,1,0:T(8,128)}), f32[4,32,128,64]{2,3,1,0:T(8,128)}) %all-gather.3.cloned.1.call-update) | async-done | bytes 4194320 | tf_op jit(solution)/shard_map/all_gather | solution.py:17
  129.9 1.6 broadcast.72
  131.6 15.4 %while.3 = (s32[]{:T(128)}, f32[32,128,64]{2,1,0:T(8,128)}, s32[]{:T(128)}, f32[4,32]{1,0:T(4,128)S(1)}, f32[4,32,128,64]{2,3,1,0:T(8,128)}, /*index=5*/s32[]{:T(128)}, s32[]{:T(128)}, s32[]{:T(128)}) while((s32[]{:T(128)}, f32[32,128,64]{2,1,0:T(8,128)}, s32[]{:T(128)}, f32[4,32]{1,0:T(4,128)S(1)}, f32[4,32,128,64]{2,3,1,0:T(8,128)}, ...), condition=%wide.region_1.2_spmd, body=%wide.region_0.1_spmd.sunk | while | flops 524293 | bytes 7340551 | solution.py:25
  131.6 1.3 constant_dynamic-slice_fusion.2
  132.9 0.6 copy.134
  133.5 3.2 %bitcast_add_fusion.3 = f32[32,128,64]{2,1,0:T(8,128)} fusion(f32[1,32,128,64]{3,2,1,0:T(8,128)S(1)} %copy.134, f32[32,128,64]{2,1,0:T(8,128)} %get-tuple-element.207, f32[32]{0:T(128)S(1)} %dynamic-slice_bitcast_fusion.2), kind=kLoop, calls=%fused_computation.clone.1 | loop fusion | flops 524288 | bytes 3145856 | tf_op jit(solution)/shard_map/while/body/add | solution.py:99
  136.7 1.3 constant_dynamic-slice_fusion.2
  138.0 0.6 copy.134
  138.6 3.2 %bitcast_add_fusion.3 = f32[32,128,64]{2,1,0:T(8,128)} fusion(f32[1,32,128,64]{3,2,1,0:T(8,128)S(1)} %copy.134, f32[32,128,64]{2,1,0:T(8,128)} %get-tuple-element.207, f32[32]{0:T(128)S(1)} %dynamic-slice_bitcast_fusion.2), kind=kLoop, calls=%fused_computation.clone.1 | loop fusion | flops 524288 | bytes 3145856 | tf_op jit(solution)/shard_map/while/body/add | solution.py:99
  141.9 1.3 constant_dynamic-slice_fusion.2
  143.2 0.6 copy.134
  143.8 3.2 %bitcast_add_fusion.3 = f32[32,128,64]{2,1,0:T(8,128)} fusion(f32[1,32,128,64]{3,2,1,0:T(8,128)S(1)} %copy.134, f32[32,128,64]{2,1,0:T(8,128)} %get-tuple-element.207, f32[32]{0:T(128)S(1)} %dynamic-slice_bitcast_fusion.2), kind=kLoop, calls=%fused_computation.clone.1 | loop fusion | flops 524288 | bytes 3145856 | tf_op jit(solution)/shard_map/while/body/add | solution.py:99
  147.0 1.9 %convert_element_type.68 = bf16[32,128,64]{2,1,0:T(8,128)(2,1)S(1)} convert(f32[32,128,64]{2,1,0:T(8,128)} %get-tuple-element.107) | non-fusion elementwise | flops 262144 | bytes 1572864 | tf_op jit(solution)/shard_map/while/body/eval_jaxpr/convert_element_type | solution.py:84
  148.9 0.2 copy-done.3
  149.2 0.0 copy-done.8
  149.2 3.1 %fusion.11 = (f32[256,2]{0,1:T(2,128)S(1)}, f32[2,16,64,256]{3,2,1,0:T(8,128)S(1)}) fusion(bf16[256,2,16,64]{0,3,2,1:T(8,128)(2,1)S(1)} %copy-done.2, f32[2,16,64,256]{3,2,1,0:T(8,128)} %fusion, bf16[256,2048]{0,1:T(8,128)(2,1)S(1)} %copy-done.3, f32[2,16]{1,0:T(2,128)S(1)} %copy-done.18, f32[256,2,16]{0,2,1:T(8,128)S(1)} %bitcast.137, ...), kind=kOutput, calls=%fused_computation.17 | convolution fusion | flops 141032960 | bytes 6981760 | tf_op jit(solution)/shard_map/while/body/eval_jaxpr/ign,gknp->igkp/dot_general | solution.py:85
  152.4 1.4 fusion.21
  153.8 0.6 copy.100
  154.4 17.3 %all_to_all.51 = bf16[4,64,2048]{2,1,0:T(8,128)(2,1)S(1)} all-to-all(bf16[4,64,2048]{2,1,0:T(8,128)(2,1)S(1)} %bitcast.118), channel_id=1, replica_groups=mesh['rollout'=2,'context'=4,'head'=4] {'head'}, dimensions={0} | all-to-all | bytes 2097152 | tf_op jit(solution)/shard_map/all_to_all | solution.py:195
  171.7 1.0 copy.110
  (47 shorter events, 0.2 us)
Async XLA Ops:
  8.3 9.7 %collective-permute-start = (bf16[4,10240]{1,0:T(4,128)(2,1)S(1)}, bf16[4,10240]{1,0:T(4,128)(2,1)S(1)}, u32[]{:S(2)}, u32[]{:S(2)}) collective-permute-start(bf16[4,10240]{1,0:T(4,128)(2,1)S(1)} %pad_maximum_fusion), channel_id=1, source_target_pairs={{0,1},{1,2},{2,3},{3,4},{4,5},{5,6},{6,7},{7,8},{8,9},{9,10},{10,1... | collective-permute-start | bytes 245768 | tf_op jit(solution)/shard_map/ppermute | solution.py:12
  16.0 3.2 %copy-start.11 = (f32[32,256]{1,0:T(8,128)}, f32[32,256]{1,0:T(8,128)S(1)}, u32[]{:S(2)}) copy-start(f32[32,256]{1,0:T(8,128)S(1)} %fusion.38) | copy-start | bytes 98308
  18.0 5.1 %copy-start.5 = (bf16[64,8192]{1,0:T(8,128)(2,1)S(1)}, bf16[64,8192]{1,0:T(8,128)(2,1)}, u32[]{:S(2)}) copy-start(bf16[64,8192]{1,0:T(8,128)(2,1)} %param.12) | copy-start | bytes 3145732
  19.2 8.5 %all-to-all-start.1 = ((bf16[64,4,512]{2,0,1:T(8,128)(2,1)}), bf16[64,4,512]{2,0,1:T(8,128)(2,1)S(1)}, u32[]{:S(2)}, u32[]{:S(2)}) async-start(bf16[64,4,512]{2,0,1:T(8,128)(2,1)} %bitcast.111), calls=%async_computation.1 | async-start | bytes 524288 | tf_op jit(solution)/shard_map/all_to_all | solution.py:136
  24.8 7.2 %copy-start.16 = (f32[32]{0:T(128)S(1)}, f32[32]{0:T(128)}, u32[]{:S(2)}) copy-start(f32[32]{0:T(128)} %param.16) | copy-start | bytes 388
  27.7 16.1 %all-to-all-start = ((bf16[64,4,2048]{2,0,1:T(8,128)(2,1)}), bf16[64,4,2048]{2,0,1:T(8,128)(2,1)S(1)}, u32[]{:S(2)}, u32[]{:S(2)}) async-start(bf16[64,4,2048]{2,0,1:T(8,128)(2,1)} %bitcast.110), calls=%async_computation | async-start | bytes 2097152 | tf_op jit(solution)/shard_map/all_to_all | solution.py:135
  32.0 98.0 %all-gather.3.cloned.1.call-start = ((), (), s32[]{:S(2)}) async-start(), calls=%async_computation.3 | async-start | bytes 5242880 | tf_op jit(solution)/shard_map/all_gather | solution.py:17
  50.2 1.2 copy-start.17
  50.2 2.7 %copy-start.10 = (f32[256,32]{1,0:T(8,128)S(1)}, f32[256,32]{1,0:T(8,128)}, u32[]{:S(2)}) copy-start(f32[256,32]{1,0:T(8,128)} %get-tuple-element.154) | copy-start | bytes 98308
  50.2 2.8 %copy-start.9 = (f32[32,256]{0,1:T(8,128)S(1)}, f32[32,256]{0,1:T(8,128)}, u32[]{:S(2)}) copy-start(f32[32,256]{0,1:T(8,128)} %get-tuple-element.158) | copy-start | bytes 98308
  50.3 3.4 %copy-start.6 = (bf16[256,2048]{1,0:T(8,128)(2,1)S(1)}, bf16[256,2048]{1,0:T(8,128)(2,1)}, u32[]{:S(2)}) copy-start(bf16[256,2048]{1,0:T(8,128)(2,1)} %param.14) | copy-start | bytes 3145732
  51.4 10.9 %copy-start.7 = (bf16[256,2,1,128]{3,2,1,0:T(2,128)(2,1)S(1)}, bf16[256,2,1,128]{3,2,1,0:T(2,128)(2,1)}, u32[]{:S(2)}) copy-start(bf16[256,2,1,128]{3,2,1,0:T(2,128)(2,1)} %get-tuple-element.147) | copy-start | bytes 393220
  63.6 1.9 %copy-start.1 = (bf16[256,2,16,64]{0,3,2,1:T(8,128)(2,1)S(1)}, bf16[256,2,16,64]{0,3,2,1:T(8,128)(2,1)}, u32[]{:S(2)}) copy-start(bf16[256,2,16,64]{0,3,2,1:T(8,128)(2,1)} %copy.90) | copy-start | bytes 3145732
  63.6 1.9 %copy-start.12 = (f32[32,256]{1,0:T(8,128)S(1)}, f32[32,256]{1,0:T(8,128)}, u32[]{:S(2)}) copy-start(f32[32,256]{1,0:T(8,128)} %copy-done.11) | copy-start | bytes 98308
  63.7 1.9 %copy-start.14 = (f32[32,256]{1,0:T(8,128)S(1)}, f32[32,256]{1,0:T(8,128)}, u32[]{:S(2)}) copy-start(f32[32,256]{1,0:T(8,128)} %copy.89) | copy-start | bytes 98308
  147.0 1.9 %copy-start.2 = (bf16[256,2,16,64]{0,3,2,1:T(8,128)(2,1)S(1)}, bf16[256,2,16,64]{0,3,2,1:T(8,128)(2,1)}, u32[]{:S(2)}) copy-start(bf16[256,2,16,64]{0,3,2,1:T(8,128)(2,1)} %copy.90) | copy-start | bytes 3145732
  147.0 2.2 %copy-start.3 = (bf16[256,2048]{0,1:T(8,128)(2,1)S(1)}, bf16[256,2048]{0,1:T(8,128)(2,1)}, u32[]{:S(2)}) copy-start(bf16[256,2048]{0,1:T(8,128)(2,1)} %copy.98) | copy-start | bytes 3145732
  147.0 2.2 %copy-start.8 = (bf16[256,2,1,128]{3,2,1,0:T(2,128)(2,1)S(1)}, bf16[256,2,1,128]{3,2,1,0:T(2,128)(2,1)}, u32[]{:S(2)}) copy-start(bf16[256,2,1,128]{3,2,1,0:T(2,128)(2,1)} %get-tuple-element.147) | copy-start | bytes 393220
  147.0 2.2 %copy-start.13 = (f32[1,256,32]{1,2,0:T(8,128)S(1)}, f32[1,256,32]{1,2,0:T(8,128)}, u32[]{:S(2)}) copy-start(f32[1,256,32]{1,2,0:T(8,128)} %copy.99) | copy-start | bytes 98308
  147.0 2.2 %copy-start.18 = (f32[2,16]{1,0:T(2,128)S(1)}, f32[2,16]{1,0:T(2,128)}, u32[]{:S(2)}) copy-start(f32[2,16]{1,0:T(2,128)} %broadcast_in_dim.64) | copy-start | bytes 388
  149.2 3.1 %copy-start = (f32[256,2048]{0,1:T(8,128)S(1)}, f32[256,2048]{0,1:T(8,128)}, u32[]{:S(2)}) copy-start(f32[256,2048]{0,1:T(8,128)} %copy.97) | copy-start | bytes 6291460
  149.2 3.1 %copy-start.4 = (f32[2,16,64,256]{3,2,1,0:T(8,128)S(1)}, f32[2,16,64,256]{3,2,1,0:T(8,128)}, u32[]{:S(2)}) copy-start(f32[2,16,64,256]{3,2,1,0:T(8,128)} %fusion) | copy-start | bytes 6291460
  149.2 3.2 %copy-start.15 = (f32[2048]{0:T(1024)S(1)}, f32[2048]{0:T(1024)}, u32[]{:S(2)}) copy-start(f32[2048]{0:T(1024)} %param.21) | copy-start | bytes 24580
Sparse Core Ops, SparseCore 0:
  51.6 78.3 all-gather.2
where the time goes:
time: 181 us; the launch traced here: 180 us
  waiting for transfers between devices  70.3 us (39%)
  local copies, waits for them, and re-layouts  29.3 us (16%)
  blocking collectives  24.5 us (14%)
  other arithmetic  18 us (10%)
  between operations  13.7 us (8%)
  matrix products  12.1 us (7%)
  starting transfers between devices  11.6 us (6%)
    all_gather x1, waiting for transfers between devices, prefix(): gathered = jax.tree.map(lambda a: lax.all_gather(a, axis), part)  59.1 us
    all_to_all x1, blocking collectives, on_device(): lax.all_to_all(head_rows, 'head', split_axis=0, concat_axis=1, tiled=True)  17.3 us
    add x3, other arithmetic, chain_combine(): later[0][:, None, None] * earlier[1] + later[1]  9.7 us
    all_to_all x1, waiting for transfers between devices, on_device(): lax.all_to_all(outgoing_inner, 'head', split_axis=1, concat_axis=0, tiled...  9.24 us
    all_gather x1, blocking collectives, prefix(): gathered = jax.tree.map(lambda a: lax.all_gather(a, axis), part)  7.27 us
    dynamic_slice x6, local copies, waits for them, and re-layouts, one(): lax.dynamic_index_in_dim(a, lap, 0, False)  5.69 us
    dot_general x1, matrix products, block_intra(): jnp.einsum('gkij,jgkp->igkp', weights, inner_view, preferred_element_type...  5.3 us
    reshape x2, local copies, waits for them, and re-layouts, block_intra(): inner_view = inner_conv.reshape(block_len, groups, per_group, head_width)  4.66 us
  transfers between devices with their start and end apart: 4, of which 3 were waited for; matrix products, arithmetic and copies ran while one was open for 13% of the time, Pallas kernels for 0%

commit v1 on v0

v1 whole, which is shorter than its diff:
```python
import functools

import jax
import jax.numpy as jnp
from jax import lax
from jax.experimental import pallas as pl
from jax.experimental.pallas import tpu as pltpu
from jax.sharding import PartitionSpec as P

BLOCK = 256
PAD = 16
CHUNK = 32
WIDE = 256
BF = jnp.bfloat16
F32 = jnp.float32


def silu(v):
    return v / (1.0 + jnp.exp(-v))


def conv_rows(src, dst, weight, first_col, cols, dst_of):
    rows = src.shape[0] - PAD
    taps = weight.shape[0] - 1

    def step(i, carry):
        r0 = pl.multiple_of(i * CHUNK, CHUNK)
        for c0 in range(0, cols, WIDE):
            raw = src[pl.ds(r0, CHUNK + PAD), c0 : c0 + WIDE].astype(F32)
            w = weight[:, pl.ds(pl.multiple_of(first_col + c0, WIDE), WIDE)]
            total = w[taps : taps + 1]
            for k in range(taps):
                o = PAD - taps + k
                total = total + w[k : k + 1] * raw[o : o + CHUNK]
            dst_of(dst, r0, c0, silu(total).astype(BF))
        return carry

    lax.fori_loop(0, rows // CHUNK, step, 0)


def store_plain(dst, r0, c0, value):
    dst[pl.ds(r0, CHUNK), c0 : c0 + WIDE] = value


def kernel(
    n, nctx, groups, heads_local,
    inner, pairs, gate, step_raw, step_bias, rate_log, skip_gain, w_inner, w_pairs, norm_gain,
    out,
    xraw, praw, xc, pc, mixed, ex, local, scores, cin, cout, outbuf,
    xs, xr, ps, pr, lsem, hs, hr, cs, cr, os, orr, olsem,
):
    me = lax.axis_index("head")
    ctx = lax.axis_index("context")
    rows = inner.shape[0]
    width = gate.shape[1]
    gw = width // groups
    per = heads_local // groups
    hd = width // heads_local
    pw = praw.shape[1]
    st = pw // (2 * groups)
    pieces = gw // WIDE

    barrier = pltpu.get_barrier_semaphore()
    for k in range(1, n):
        pl.semaphore_signal(barrier, inc=1, device_id={"head": lax.rem(me + k, n)})

    @pl.when(ctx > 0)
    def _():
        pl.semaphore_signal(barrier, inc=1, device_id={"context": ctx - 1})

    @pl.when(ctx < nctx - 1)
    def _():
        pl.semaphore_signal(barrier, inc=1, device_id={"context": ctx + 1})

    links = jnp.where(ctx > 0, 1, 0) + jnp.where(ctx < nctx - 1, 1, 0)
    pl.semaphore_wait(barrier, n - 1 + links)

    def p_copy(k, who, at):
        return pltpu.make_async_remote_copy(
            src_ref=pairs.at[:, pl.ds(pl.multiple_of(who * pw, 128), pw)],
            dst_ref=praw.at[pl.ds(pl.multiple_of(PAD + at * rows, 16), rows), :],
            send_sem=ps.at[k - 1], recv_sem=pr.at[k - 1], device_id={"head": who})

    def x_copy(g, k, who, at):
        return pltpu.make_async_remote_copy(
            src_ref=inner.at[:, pl.ds(pl.multiple_of(who * width + g * gw, 128), gw)],
            dst_ref=xraw.at[g, pl.ds(pl.multiple_of(PAD + at * rows, 16), rows), :],
            send_sem=xs.at[g, k - 1], recv_sem=xr.at[g, k - 1], device_id={"head": who})

    def o_copy(g, k, who, at):
        return pltpu.make_async_remote_copy(
            src_ref=outbuf.at[g, pl.ds(pl.multiple_of(who * rows, 16), rows), :],
            dst_ref=out.at[:, pl.ds(pl.multiple_of(at * width + g * gw, 128), gw)],
            send_sem=os.at[g, k - 1], recv_sem=orr.at[g, k - 1], device_id={"head": who})

    def halo(i, ref):
        last = ref.shape[0] - PAD
        return pltpu.make_async_remote_copy(
            src_ref=ref.at[last:, :], dst_ref=ref.at[0:PAD, :],
            send_sem=hs.at[i], recv_sem=hr.at[i],
            device_id={"context": lax.rem(ctx + 1, nctx)})

    def chain(g, p):
        return pltpu.make_async_remote_copy(
            src_ref=cout.at[g, p], dst_ref=cin.at[g, p],
            send_sem=cs.at[g, p], recv_sem=cr.at[g, p],
            device_id={"context": lax.rem(ctx + 1, nctx)})

    def to(k):
        return lax.rem(me + k, n)

    def source(k):
        return lax.rem(me + n - k, n)

    for k in range(1, n):
        p_copy(k, to(k), me).start()
    for g in range(groups):
        for k in range(1, n):
            x_copy(g, k, to(k), me).start()
    own_rows = pl.ds(pl.multiple_of(PAD + me * rows, 16), rows)
    own = [pltpu.make_async_copy(
        pairs.at[:, pl.ds(pl.multiple_of(me * pw, 128), pw)], praw.at[own_rows, :], lsem.at[0])]
    for g in range(groups):
        own.append(pltpu.make_async_copy(
            inner.at[:, pl.ds(pl.multiple_of(me * width + g * gw, 128), gw)],
            xraw.at[g, own_rows, :], lsem.at[1 + g]))
    for c in own:
        c.start()

    @pl.when(ctx == 0)
    def _():
        praw[0:PAD, :] = jnp.zeros((PAD, pw), BF)
        for g in range(groups):
            xraw[g, 0:PAD, :] = jnp.zeros((PAD, gw), BF)

    v = step_raw[...].astype(F32) + step_bias[...]
    step = jnp.maximum(v, 0.0) + jnp.log1p(jnp.exp(-jnp.abs(v)))
    tri_r = lax.broadcasted_iota(jnp.int32, (BLOCK, BLOCK), 0)
    tri_c = lax.broadcasted_iota(jnp.int32, (BLOCK, BLOCK), 1)
    lower = tri_r >= tri_c
    lc = jnp.dot(lower.astype(F32), -jnp.exp(rate_log[...]) * step,
                 precision=lax.Precision.HIGHEST, preferred_element_type=F32)
    shifted = lc - jnp.log(step)
    shifted_t = shifted.T
    tail = jnp.exp(lc[BLOCK - 1 : BLOCK, :] - shifted)
    grow = jnp.exp(lc)

    def spread(cols, a):
        left = lax.broadcasted_iota(jnp.int32, (cols.shape[0], 2 * hd), 1) < hd
        return jnp.where(left, cols[:, a : a + 1], cols[:, a + 1 : a + 2])

    def arrived(i, ref, waits, own_copy):
        for w in waits:
            w.wait_recv()
        own_copy.wait()

        @pl.when(ctx < nctx - 1)
        def _():
            halo(i, ref).start()

        @pl.when(ctx > 0)
        def _():
            halo(i, ref).wait_recv()

    for g in range(groups):
        for a in range(0, per, 2):
            ex[g, :, a * hd : (a + 2) * hd] = spread(grow, g * per + a)

    arrived(0, praw, [p_copy(k, to(k), source(k)) for k in range(1, n)], own[0])
    conv_rows(praw, pc, w_pairs, me * pw, pw, store_plain)
    bts = []
    for g in range(groups):
        bt = pc[:, 2 * g * st : (2 * g + 1) * st].astype(F32).T.astype(BF)
        bts.append(bt)
        raw_scores = jnp.dot(
            pc[:, (2 * g + 1) * st : (2 * g + 2) * st], bt, preferred_element_type=F32)
        scores[g] = jnp.where(lower, raw_scores, 0.0)

    def prepare(g):
        arrived(1 + g, xraw.at[g],
                [x_copy(g, k, to(k), source(k)) for k in range(1, n)], own[1 + g])
        conv_rows(xraw.at[g], xc.at[g], w_inner, me * width + g * gw, gw, store_plain)
        for p in range(pieces):
            parts = []
            for a in range(p * WIDE // hd, (p + 1) * WIDE // hd, 2):
                x = xc[g, :, a * hd : (a + 2) * hd].astype(F32)
                parts.append((x * spread(tail, g * per + a)).astype(BF))
            weighted = jnp.concatenate(parts, axis=1)
            local[g, p] = jnp.dot(bts[g], weighted, preferred_element_type=F32)

            @pl.when(ctx == 0)
            def _():
                cout[g, p] = local[g, p].astype(BF)
                if nctx > 1:
                    chain(g, p).start()

    half = BLOCK // 2

    def intra(g, a):
        x = xc[g, :, a * hd : (a + 2) * hd]
        top, low = [], []
        for b in (a, a + 1):
            h = g * per + b
            col = lc[:, h : h + 1]
            row = shifted_t[h : h + 1, :]
            w0 = scores[g, :half, :half] * jnp.exp(jnp.minimum(col[:half] - row[:, :half], 30.0))
            top.append(jnp.dot(w0.astype(BF), x[:half], preferred_element_type=F32))
            w1 = scores[g, half:, :] * jnp.exp(jnp.minimum(col[half:] - row, 30.0))
            low.append(jnp.dot(w1.astype(BF), x, preferred_element_type=F32))
        left = lax.broadcasted_iota(jnp.int32, (half, 2 * hd), 1) < hd
        gain = spread(skip_gain[...], g * per + a)
        xf = x.astype(F32) * gain
        mixed[g, :half, a * hd : (a + 2) * hd] = jnp.where(left, top[0], top[1]) + xf[:half]
        mixed[g, half:, a * hd : (a + 2) * hd] = jnp.where(left, low[0], low[1]) + xf[half:]

    def serve(g, p):
        cols = slice(p * WIDE, (p + 1) * WIDE)

        @pl.when(ctx > 0)
        def _():
            chain(g, p).wait_recv()
            held = cin[g, p]

            @pl.when(ctx < nctx - 1)
            def _():
                decay = ex[g, BLOCK - 1 : BLOCK, cols]
                cout[g, p] = (decay * held.astype(F32) + local[g, p]).astype(BF)
                chain(g, p).start()

            cmat = pc[:, (2 * g + 1) * st : (2 * g + 2) * st]
            carried = jnp.dot(cmat, held, preferred_element_type=F32)
            mixed[g, :, cols] = mixed[g, :, cols] + carried * ex[g, :, cols]

    def work(g):
        for p in range(pieces):
            for a in range(p * WIDE // hd, (p + 1) * WIDE // hd, 2):
                intra(g, a)
            serve(g, p)

    own_out = []

    def finish(g):
        for k in list(range(1, n)) + [0]:
            who = to(k)
            rs = pl.ds(pl.multiple_of(who * rows, rows), rows)
            ssq = jnp.zeros((rows, 1), F32)
            for p in range(pieces):
                cols = slice(p * WIDE, (p + 1) * WIDE)
                z = gate[rs, g * gw + p * WIDE : g * gw + (p + 1) * WIDE].astype(F32)
                gated = mixed[g, rs, cols] * silu(z)
                mixed[g, rs, cols] = gated
                ssq = ssq + jnp.sum(gated * gated, axis=1, keepdims=True)
            inv = lax.rsqrt(ssq / gw + 1e-05)
            for p in range(pieces):
                cols = slice(p * WIDE, (p + 1) * WIDE)
                gain = norm_gain[:, g * gw + p * WIDE : g * gw + (p + 1) * WIDE]
                outbuf[g, rs, cols] = (mixed[g, rs, cols] * inv * gain).astype(BF)
            if k:
                o_copy(g, k, who, me).start()
            else:
                c = pltpu.make_async_copy(
                    outbuf.at[g, rs, :],
                    out.at[:, pl.ds(pl.multiple_of(me * width + g * gw, 128), gw)], olsem.at[g])
                c.start()
                own_out.append(c)

    prepare(0)
    work(0)
    for g in range(1, groups):
        prepare(g)
        finish(g - 1)
        work(g)
    finish(groups - 1)

    for k in range(1, n):
        p_copy(k, to(k), me).wait_send()
        for g in range(groups):
            x_copy(g, k, to(k), me).wait_send()
            o_copy(g, k, to(k), me).wait_send()
            o_copy(g, k, to(k), source(k)).wait_recv()
    for c in own_out:
        c.wait()

    @pl.when(ctx < nctx - 1)
    def _():
        halo(0, praw).wait_send()
        for g in range(groups):
            halo(1 + g, xraw.at[g]).wait_send()
            for p in range(pieces):
                chain(g, p).wait_send()


def on_device(
    inner_raw, pairs_raw, gate_raw, step_raw, step_bias, rate_log,
    skip_gain, conv_inner, conv_pairs, norm_gain,
):
    n = lax.axis_size("head")
    nctx = lax.axis_size("context")
    rows, full = inner_raw.shape
    width = gate_raw.shape[1]
    heads = step_raw.shape[1]
    groups = pairs_raw.shape[1] // n
    st = pairs_raw.shape[3]
    pw = groups * 2 * st
    gw = width // groups
    pieces = gw // WIDE
    pairs = pairs_raw.reshape(rows, -1)
    w_pairs = conv_pairs.reshape(conv_pairs.shape[0], -1)
    vm = pl.BlockSpec(memory_space=pltpu.VMEM)
    hbm = pl.BlockSpec(memory_space=pl.ANY)
    dma = pltpu.SemaphoreType.DMA
    return pl.pallas_call(
        functools.partial(kernel, n, nctx, groups, heads),
        out_shape=jax.ShapeDtypeStruct((rows, full), BF),
        in_specs=[hbm, hbm] + [vm] * 8,
        out_specs=hbm,
        scratch_shapes=[
            pltpu.VMEM((groups, PAD + BLOCK, gw), BF),
            pltpu.VMEM((PAD + BLOCK, pw), BF),
            pltpu.VMEM((groups, BLOCK, gw), BF),
            pltpu.VMEM((BLOCK, pw), BF),
            pltpu.VMEM((groups, BLOCK, gw), F32),
            pltpu.VMEM((groups, BLOCK, gw), F32),
            pltpu.VMEM((groups, pieces, st, WIDE), F32),
            pltpu.VMEM((groups, BLOCK, BLOCK), F32),
            pltpu.VMEM((groups, pieces, st, WIDE), BF),
            pltpu.VMEM((groups, pieces, st, WIDE), BF),
            pltpu.VMEM((groups, BLOCK, gw), BF),
            dma((groups, n - 1)), dma((groups, n - 1)),
            dma((n - 1,)), dma((n - 1,)),
            dma((1 + groups,)),
            dma((1 + groups,)), dma((1 + groups,)),
            dma((groups, pieces)), dma((groups, pieces)),
            dma((groups, n - 1)), dma((groups, n - 1)),
            dma((groups,)),
        ],
        compiler_params=pltpu.CompilerParams(
            collective_id=0, has_side_effects=True, vmem_limit_bytes=40 * 1024 * 1024),
        cost_estimate=pl.CostEstimate(
            flops=700_000_000, bytes_accessed=4_000_000, transcendentals=4_000_000),
        name="mixer",
    )(
        inner_raw, pairs, gate_raw, step_raw, step_bias[None, :], rate_log[None, :],
        skip_gain[None, :], conv_inner, w_pairs, norm_gain[None, :],
    )


def solution(mesh):
    placed = (
        P(("rollout", "context", "head"), None),
        P(("rollout", "context", "head"), None, None, None),
        P(("rollout", "context"), "head"),
        P(("rollout", "context"), "head"),
        P("head"),
        P("head"),
        P("head"),
        P(),
        P(),
        P("head"),
    )
    return jax.shard_map(
        on_device,
        mesh=mesh,
        in_specs=placed,
        out_specs=P(("rollout", "context", "head"), None),
        check_vma=False,
    )
```

time: 181 us -> 48.5 us (0.27)
  waiting for transfers between devices: 70.3 us -> 0 us
  Pallas kernels: 0 us -> 42.6 us
  blocking collectives: 24.5 us -> 0 us
  local copies, waits for them, and re-layouts: 29.3 us -> 5.54 us
  other arithmetic: 18 us -> 0 us
  between operations: 13.7 us -> 0.12 us
  matrix products: 12.1 us -> 0 us
  starting transfers between devices: 11.6 us -> 0 us
    all_gather x1 -> x0, waiting for transfers between devices: 59.1 us -> none  [prefix(): gathered = jax.tree.map(lambda a: lax.all_gather(a, axis), part)]
    pallas_call x0 -> x1, Pallas kernels: none -> 42.6 us  [on_device(): pl.pallas_call(functools.partial(kernel, n, nctx, groups, heads), out_sha...]
    all_to_all x1 -> x0, blocking collectives: 17.3 us -> none  [on_device(): lax.all_to_all(head_rows, 'head', split_axis=0, concat_axis=1, tiled=True)]
    dot_general x5 -> x0, matrix products: 12.1 us -> none  [the longest x1 5.3 us: block_intra(): jnp.einsum('gkij,jgkp->igkp', weights, inner_view, preferred_element_type...]
    all_to_all x2 -> x0, waiting for transfers between devices: 11.1 us -> none  [the longest x1 9.24 us: on_device(): lax.all_to_all(outgoing_inner, 'head', split_axis=1, concat_axis=0, tiled...]
    add x4 -> x0, other arithmetic: 10.9 us -> none  [the longest x3 9.7 us: chain_combine(): later[0][:, None, None] * earlier[1] + later[1]]
    all_to_all x2 -> x0, starting transfers between devices: 8.15 us -> none  [the longest x1 4.24 us: on_device(): lax.all_to_all(outgoing_inner, 'head', split_axis=1, concat_axis=0, tiled...]
    all_gather x1 -> x0, blocking collectives: 7.27 us -> none  [prefix(): gathered = jax.tree.map(lambda a: lax.all_gather(a, axis), part)]
  transfers between devices with their start and end apart: 4 -> 0, of which waited for: 3 -> 0; matrix products, arithmetic and copies ran while one was open for 13% -> 0% of each run, Pallas kernels for 0% -> 0%
where the time goes in v1:
time: 48.5 us; the launch traced here: 48.3 us
  Pallas kernels  42.6 us (88%)
  local copies, waits for them, and re-layouts  5.54 us (11%)
    pallas_call x1, Pallas kernels, on_device(): pl.pallas_call(functools.partial(kernel, n, nctx, groups, heads), out_sha...  42.6 us
    unnamed x18, local copies, waits for them, and re-layouts  4.29 us
    reshape x1, local copies, waits for them, and re-layouts, on_device(): pairs = pairs_raw.reshape(rows, -1)  1.22 us

profile of v1, /device:TPU:26, one launch (start us, length us, event | category | flops | bytes accessed | tf_op | source)
XLA Modules:
  0.0 48.3 jit_solution(10442424761467344925)
XLA Ops:
  0.0 0.0 copy-start.7
  0.0 0.8 %copy.11.step_raw = bf16[256,32]{1,0:T(8,128)(2,1)S(1)} copy(bf16[256,32]{0,1:T(8,128)(2,1)} %param.13) | data formatting | bytes 32768 | tf_op args[3]
  0.8 0.0 copy-done.7
  0.9 0.0 copy-start.2
  0.9 0.0 copy-start.3
  0.9 0.0 copy-start.4
  0.9 0.0 copy-start.5
  0.9 0.0 copy-start.6
  1.0 1.2 %reshape.6.pairs = bf16[64,2048]{1,0:T(8,128)(2,1)S(1)} reshape(bf16[64,8,2,128]{3,2,1,0:T(2,128)(2,1)} %param.11) | data formatting | bytes 524288 | tf_op jit(solution)/shard_map/reshape | solution.py:307
  2.2 0.0 copy-done.2
  2.2 0.0 copy-done.3
  2.2 0.0 copy-done.4
  2.2 0.0 copy-done.5
  2.2 0.0 copy-done.6
  2.2 0.0 copy-start
  2.2 1.2 %copy-done = bf16[64,8192]{1,0:T(8,128)(2,1)S(1)} copy-done((bf16[64,8192]{1,0:T(8,128)(2,1)S(1)}, bf16[64,8192]{1,0:T(8,128)(2,1)}, u32[]{:S(2)}) %copy-start) | copy-done | bytes 1048600
  3.5 0.0 copy-start.1
  3.5 1.2 %copy-done.1 = bf16[256,2048]{1,0:T(8,128)(2,1)S(1)} copy-done((bf16[256,2048]{1,0:T(8,128)(2,1)S(1)}, bf16[256,2048]{1,0:T(8,128)(2,1)}, u32[]{:S(2)}) %copy-start.1) | copy-done | bytes 1048600
  4.7 42.6 %mixer.1 = bf16[64,8192]{1,0:T(8,128)(2,1)S(1)} custom-call(bf16[64,8192]{1,0:T(8,128)(2,1)S(1)} %copy-done, bf16[64,2048]{1,0:T(8,128)(2,1)S(1)} %reshape.6.pairs, bf16[256,2048]{1,0:T(8,128)(2,1)S(1)} %copy-done.1, bf16[256,32]{1,0:T(8,128)(2,1)S(1)} %copy.11.step_raw, f32[1,32]{1,0:T(1,128)S(1)} %bitcast.5, f32[1,32]{1,0:T(1,128)S(1)} %bitcast.6, ...), custom_call_target="tpu_custom_call" | custom-call | flops 700000000 | bytes 4000000 | tf_op jit(solution)/shard_map/mixer/pallas_call | solution.py:312
  47.3 1.0 %copy.13 = bf16[64,8192]{1,0:T(8,128)(2,1)} copy(bf16[64,8192]{1,0:T(8,128)(2,1)S(1)} %mixer.1) | data formatting | bytes 2097152
  (1 shorter events, 0.0 us)
Async XLA Ops:
  0.0 0.8 %copy-start.7 = (f32[5,8,2,128]{3,2,1,0:T(2,128)S(1)}, f32[5,8,2,128]{3,2,1,0:T(2,128)}, u32[]{:S(2)}) copy-start(f32[5,8,2,128]{3,2,1,0:T(2,128)} %param.18) | copy-start | bytes 122884
  0.9 1.3 %copy-start.2 = (f32[5,8192]{1,0:T(8,128)S(1)}, f32[5,8192]{1,0:T(8,128)}, u32[]{:S(2)}) copy-start(f32[5,8192]{1,0:T(8,128)} %w_inner.1) | copy-start | bytes 491524
  0.9 1.3 %copy-start.3 = (f32[2048]{0:T(1024)S(1)}, f32[2048]{0:T(1024)}, u32[]{:S(2)}) copy-start(f32[2048]{0:T(1024)} %param.19) | copy-start | bytes 24580
  0.9 1.3 %copy-start.4 = (f32[32]{0:T(128)S(1)}, f32[32]{0:T(128)}, u32[]{:S(2)}) copy-start(f32[32]{0:T(128)} %param.14) | copy-start | bytes 388
  0.9 1.3 %copy-start.5 = (f32[32]{0:T(128)S(1)}, f32[32]{0:T(128)}, u32[]{:S(2)}) copy-start(f32[32]{0:T(128)} %param.15) | copy-start | bytes 388
  0.9 1.3 %copy-start.6 = (f32[32]{0:T(128)S(1)}, f32[32]{0:T(128)}, u32[]{:S(2)}) copy-start(f32[32]{0:T(128)} %param.16) | copy-start | bytes 388
  2.2 1.2 %copy-start = (bf16[64,8192]{1,0:T(8,128)(2,1)S(1)}, bf16[64,8192]{1,0:T(8,128)(2,1)}, u32[]{:S(2)}) copy-start(bf16[64,8192]{1,0:T(8,128)(2,1)} %inner.1) | copy-start | bytes 3145732
  3.5 1.2 %copy-start.1 = (bf16[256,2048]{1,0:T(8,128)(2,1)S(1)}, bf16[256,2048]{1,0:T(8,128)(2,1)}, u32[]{:S(2)}) copy-start(bf16[256,2048]{1,0:T(8,128)(2,1)} %gate.1) | copy-start | bytes 3145732

commit v2 on v1

--- a/solution.py
+++ b/solution.py
@@ -11,6 +11,7 @@
 PAD = 16
 CHUNK = 32
 WIDE = 256
+PIECE = 512
 BF = jnp.bfloat16
 F32 = jnp.float32
 
@@ -44,21 +45,26 @@
 
 def kernel(
     n, nctx, groups, heads_local,
-    inner, pairs, gate, step_raw, step_bias, rate_log, skip_gain, w_inner, w_pairs, norm_gain,
+    inner, pairs, gate_hbm, step_raw, step_bias, rate_log, skip_gain, w_inner, w_pairs, norm_gain,
     out,
-    xraw, praw, xc, pc, mixed, ex, local, scores, cin, cout, outbuf,
-    xs, xr, ps, pr, lsem, hs, hr, cs, cr, os, orr, olsem,
+    gbuf, xraw, praw, xc, pc, mixed, ex, local, scores, cin, cout, outbuf,
+    xs, xr, ps, pr, lsem, hs, hr, cs, cr, os, orr, olsem, gsem,
 ):
     me = lax.axis_index("head")
     ctx = lax.axis_index("context")
     rows = inner.shape[0]
-    width = gate.shape[1]
+    width = gate_hbm.shape[1]
+    gate = gbuf
     gw = width // groups
     per = heads_local // groups
     hd = width // heads_local
     pw = praw.shape[1]
     st = pw // (2 * groups)
     pieces = gw // WIDE
+    count = width // PIECE
+
+    gate_copy = pltpu.make_async_copy(gate_hbm, gbuf, gsem)
+    gate_copy.start()
 
     barrier = pltpu.get_barrier_semaphore()
     for k in range(1, n):
@@ -81,11 +87,11 @@
             dst_ref=praw.at[pl.ds(pl.multiple_of(PAD + at * rows, 16), rows), :],
             send_sem=ps.at[k - 1], recv_sem=pr.at[k - 1], device_id={"head": who})
 
-    def x_copy(g, k, who, at):
-        return pltpu.make_async_remote_copy(
-            src_ref=inner.at[:, pl.ds(pl.multiple_of(who * width + g * gw, 128), gw)],
-            dst_ref=xraw.at[g, pl.ds(pl.multiple_of(PAD + at * rows, 16), rows), :],
-            send_sem=xs.at[g, k - 1], recv_sem=xr.at[g, k - 1], device_id={"head": who})
+    def x_copy(q, k, who, at):
+        return pltpu.make_async_remote_copy(
+            src_ref=inner.at[:, pl.ds(pl.multiple_of(who * width + q * PIECE, 128), PIECE)],
+            dst_ref=xraw.at[q, pl.ds(pl.multiple_of(PAD + at * rows, 16), rows), :],
+            send_sem=xs.at[q, k - 1], recv_sem=xr.at[q, k - 1], device_id={"head": who})
 
     def o_copy(g, k, who, at):
         return pltpu.make_async_remote_copy(
@@ -114,34 +120,35 @@
 
     for k in range(1, n):
         p_copy(k, to(k), me).start()
-    for g in range(groups):
+    for q in range(count):
         for k in range(1, n):
-            x_copy(g, k, to(k), me).start()
+            x_copy(q, k, to(k), me).start()
     own_rows = pl.ds(pl.multiple_of(PAD + me * rows, 16), rows)
     own = [pltpu.make_async_copy(
         pairs.at[:, pl.ds(pl.multiple_of(me * pw, 128), pw)], praw.at[own_rows, :], lsem.at[0])]
-    for g in range(groups):
+    for q in range(count):
         own.append(pltpu.make_async_copy(
-            inner.at[:, pl.ds(pl.multiple_of(me * width + g * gw, 128), gw)],
-            xraw.at[g, own_rows, :], lsem.at[1 + g]))
+            inner.at[:, pl.ds(pl.multiple_of(me * width + q * PIECE, 128), PIECE)],
+            xraw.at[q, own_rows, :], lsem.at[1 + q]))
     for c in own:
         c.start()
 
     @pl.when(ctx == 0)
     def _():
         praw[0:PAD, :] = jnp.zeros((PAD, pw), BF)
-        for g in range(groups):
-            xraw[g, 0:PAD, :] = jnp.zeros((PAD, gw), BF)
-
-    v = step_raw[...].astype(F32) + step_bias[...]
+        for q in range(count):
+            xraw[q, 0:PAD, :] = jnp.zeros((PAD, PIECE), BF)
+
+    v = step_raw[...].astype(F32) + step_bias[...].T
     step = jnp.maximum(v, 0.0) + jnp.log1p(jnp.exp(-jnp.abs(v)))
     tri_r = lax.broadcasted_iota(jnp.int32, (BLOCK, BLOCK), 0)
     tri_c = lax.broadcasted_iota(jnp.int32, (BLOCK, BLOCK), 1)
     lower = tri_r >= tri_c
-    lc = jnp.dot(lower.astype(F32), -jnp.exp(rate_log[...]) * step,
-                 precision=lax.Precision.HIGHEST, preferred_element_type=F32)
-    shifted = lc - jnp.log(step)
-    shifted_t = shifted.T
+    lc_t = jnp.dot(-jnp.exp(rate_log[...].T) * step, (tri_r <= tri_c).astype(F32),
+                   precision=lax.Precision.HIGHEST, preferred_element_type=F32)
+    shifted_t = lc_t - jnp.log(step)
+    lc = lc_t.T
+    shifted = shifted_t.T
     tail = jnp.exp(lc[BLOCK - 1 : BLOCK, :] - shifted)
     grow = jnp.exp(lc)
 
@@ -176,28 +183,32 @@
             pc[:, (2 * g + 1) * st : (2 * g + 2) * st], bt, preferred_element_type=F32)
         scores[g] = jnp.where(lower, raw_scores, 0.0)
 
-    def prepare(g):
-        arrived(1 + g, xraw.at[g],
-                [x_copy(g, k, to(k), source(k)) for k in range(1, n)], own[1 + g])
-        conv_rows(xraw.at[g], xc.at[g], w_inner, me * width + g * gw, gw, store_plain)
-        for p in range(pieces):
+    def prepare(q):
+        arrived(1 + q, xraw.at[q],
+                [x_copy(q, k, to(k), source(k)) for k in range(1, n)], own[1 + q])
+        conv_rows(xraw.at[q], xc.at[q], w_inner, me * width + q * PIECE, PIECE, store_plain)
+        for c0 in range(0, PIECE, WIDE):
+            g, first = divmod(q * PIECE + c0, gw)
+            p = first // WIDE
             parts = []
-            for a in range(p * WIDE // hd, (p + 1) * WIDE // hd, 2):
-                x = xc[g, :, a * hd : (a + 2) * hd].astype(F32)
-                parts.append((x * spread(tail, g * per + a)).astype(BF))
+            for o in range(c0, c0 + WIDE, 2 * hd):
+                x = xc[q, :, o : o + 2 * hd].astype(F32)
+                parts.append((x * spread(tail, (q * PIECE + o) // hd)).astype(BF))
             weighted = jnp.concatenate(parts, axis=1)
-            local[g, p] = jnp.dot(bts[g], weighted, preferred_element_type=F32)
+            state = jnp.dot(bts[g], weighted, preferred_element_type=F32)
+            local[g, p] = state
 
             @pl.when(ctx == 0)
             def _():
-                cout[g, p] = local[g, p].astype(BF)
+                cout[g, p] = state.astype(BF)
                 if nctx > 1:
                     chain(g, p).start()
 
     half = BLOCK // 2
 
     def intra(g, a):
-        x = xc[g, :, a * hd : (a + 2) * hd]
+        q, o = divmod(g * gw + a * hd, PIECE)
+        x = xc[q, :, o : o + 2 * hd]
         top, low = [], []
         for b in (a, a + 1):
             h = g * per + b
@@ -213,29 +224,27 @@
         mixed[g, :half, a * hd : (a + 2) * hd] = jnp.where(left, top[0], top[1]) + xf[:half]
         mixed[g, half:, a * hd : (a + 2) * hd] = jnp.where(left, low[0], low[1]) + xf[half:]
 
-    def serve(g, p):
-        cols = slice(p * WIDE, (p + 1) * WIDE)
-
+    def forward(g, p):
+        @pl.when(jnp.logical_and(ctx > 0, ctx < nctx - 1))
+        def _():
+            chain(g, p).wait_recv()
+            decay = ex[g, BLOCK - 1 : BLOCK, p * WIDE : (p + 1) * WIDE]
+            cout[g, p] = (decay * cin[g, p].astype(F32) + local[g, p]).astype(BF)
+            chain(g, p).start()
+
+    def absorb(g):
         @pl.when(ctx > 0)
         def _():
-            chain(g, p).wait_recv()
-            held = cin[g, p]
-
-            @pl.when(ctx < nctx - 1)
-            def _():
-                decay = ex[g, BLOCK - 1 : BLOCK, cols]
-                cout[g, p] = (decay * held.astype(F32) + local[g, p]).astype(BF)
-                chain(g, p).start()
-
-            cmat = pc[:, (2 * g + 1) * st : (2 * g + 2) * st]
-            carried = jnp.dot(cmat, held, preferred_element_type=F32)
-            mixed[g, :, cols] = mixed[g, :, cols] + carried * ex[g, :, cols]
-
-    def work(g):
-        for p in range(pieces):
-            for a in range(p * WIDE // hd, (p + 1) * WIDE // hd, 2):
-                intra(g, a)
-            serve(g, p)
+            for p in range(pieces):
+                cols = slice(p * WIDE, (p + 1) * WIDE)
+
+                @pl.when(ctx == nctx - 1)
+                def _():
+                    chain(g, p).wait_recv()
+
+                cmat = pc[:, (2 * g + 1) * st : (2 * g + 2) * st]
+                carried = jnp.dot(cmat, cin[g, p], preferred_element_type=F32)
+                mixed[g, :, cols] = mixed[g, :, cols] + carried * ex[g, :, cols]
 
     own_out = []
 
@@ -264,18 +273,23 @@
                 c.start()
                 own_out.append(c)
 
-    prepare(0)
-    work(0)
-    for g in range(1, groups):
-        prepare(g)
-        finish(g - 1)
-        work(g)
-    finish(groups - 1)
+    for q in range(count):
+        prepare(q)
+        for c0 in range(q * PIECE, (q + 1) * PIECE, WIDE):
+            g, first = divmod(c0, gw)
+            for a in range(first // hd, (first + WIDE) // hd, 2):
+                intra(g, a)
+            forward(g, first // WIDE)
+    gate_copy.wait()
+    for g in range(groups):
+        absorb(g)
+        finish(g)
 
     for k in range(1, n):
         p_copy(k, to(k), me).wait_send()
+        for q in range(count):
+            x_copy(q, k, to(k), me).wait_send()
         for g in range(groups):
-            x_copy(g, k, to(k), me).wait_send()
             o_copy(g, k, to(k), me).wait_send()
             o_copy(g, k, to(k), source(k)).wait_recv()
     for c in own_out:
@@ -284,8 +298,9 @@
     @pl.when(ctx < nctx - 1)
     def _():
         halo(0, praw).wait_send()
+        for q in range(count):
+            halo(1 + q, xraw.at[q]).wait_send()
         for g in range(groups):
-            halo(1 + g, xraw.at[g]).wait_send()
             for p in range(pieces):
                 chain(g, p).wait_send()
 
@@ -304,20 +319,23 @@
     pw = groups * 2 * st
     gw = width // groups
     pieces = gw // WIDE
+    count = width // PIECE
     pairs = pairs_raw.reshape(rows, -1)
     w_pairs = conv_pairs.reshape(conv_pairs.shape[0], -1)
     vm = pl.BlockSpec(memory_space=pltpu.VMEM)
     hbm = pl.BlockSpec(memory_space=pl.ANY)
+    far = pl.BlockSpec(memory_space=pltpu.MemorySpace.HBM)
     dma = pltpu.SemaphoreType.DMA
     return pl.pallas_call(
         functools.partial(kernel, n, nctx, groups, heads),
         out_shape=jax.ShapeDtypeStruct((rows, full), BF),
-        in_specs=[hbm, hbm] + [vm] * 8,
+        in_specs=[far, hbm, far] + [vm] * 7,
         out_specs=hbm,
         scratch_shapes=[
-            pltpu.VMEM((groups, PAD + BLOCK, gw), BF),
+            pltpu.VMEM((BLOCK, width), BF),
+            pltpu.VMEM((count, PAD + BLOCK, PIECE), BF),
             pltpu.VMEM((PAD + BLOCK, pw), BF),
-            pltpu.VMEM((groups, BLOCK, gw), BF),
+            pltpu.VMEM((count, BLOCK, PIECE), BF),
             pltpu.VMEM((BLOCK, pw), BF),
             pltpu.VMEM((groups, BLOCK, gw), F32),
             pltpu.VMEM((groups, BLOCK, gw), F32),
@@ -326,13 +344,14 @@
             pltpu.VMEM((groups, pieces, st, WIDE), BF),
             pltpu.VMEM((groups, pieces, st, WIDE), BF),
             pltpu.VMEM((groups, BLOCK, gw), BF),
-            dma((groups, n - 1)), dma((groups, n - 1)),
+            dma((count, n - 1)), dma((count, n - 1)),
             dma((n - 1,)), dma((n - 1,)),
-            dma((1 + groups,)),
-            dma((1 + groups,)), dma((1 + groups,)),
+            dma((1 + count,)),
+            dma((1 + count,)), dma((1 + count,)),
             dma((groups, pieces)), dma((groups, pieces)),
             dma((groups, n - 1)), dma((groups, n - 1)),
             dma((groups,)),
+            dma,
         ],
         compiler_params=pltpu.CompilerParams(
             collective_id=0, has_side_effects=True, vmem_limit_bytes=40 * 1024 * 1024),
@@ -340,7 +359,7 @@
             flops=700_000_000, bytes_accessed=4_000_000, transcendentals=4_000_000),
         name="mixer",
     )(
-        inner_raw, pairs, gate_raw, step_raw, step_bias[None, :], rate_log[None, :],
+        inner_raw, pairs, gate_raw, step_raw.T, step_bias[None, :], rate_log[None, :],
         skip_gain[None, :], conv_inner, w_pairs, norm_gain[None, :],
     )
 

time: 48.5 us -> 49.7 us (1.025)
  Pallas kernels: 42.6 us -> 43.8 us
    pallas_call x1, Pallas kernels: 42.6 us -> 43.8 us  [on_device(): pl.pallas_call(functools.partial(kernel, n, nctx, groups, heads), out_sha...]
    unnamed x18 -> x17, local copies, waits for them, and re-layouts: 4.29 us -> 3.45 us
    reshape x1, local copies, waits for them, and re-layouts: 0.03 us -> 0.81 us  [on_device(): w_pairs = conv_pairs.reshape(conv_pairs.shape[0], -1)]
where the time goes in v2:
time: 49.7 us; the launch traced here: 49.4 us
  Pallas kernels  43.8 us (88%)
  local copies, waits for them, and re-layouts  5.48 us (11%)
    pallas_call x1, Pallas kernels, on_device(): pl.pallas_call(functools.partial(kernel, n, nctx, groups, heads), out_sha...  43.8 us
    unnamed x17, local copies, waits for them, and re-layouts  3.45 us
    reshape x1, local copies, waits for them, and re-layouts, on_device(): pairs = pairs_raw.reshape(rows, -1)  1.22 us

profile of v2, /device:TPU:26, one launch (start us, length us, event | category | flops | bytes accessed | tf_op | source)
XLA Modules:
  0.0 49.4 jit_solution(7048736184019966118)
XLA Ops:
  0.0 0.8 %reshape.7.w_pairs = f32[5,2048]{1,0:T(8,128)S(1)} reshape(f32[5,8,2,128]{3,2,1,0:T(2,128)} %param.18) | data formatting | bytes 81920 | tf_op jit(solution)/shard_map/reshape | solution.py:324
  0.8 0.0 copy-start.2
  0.8 0.0 copy-start.3
  0.8 0.0 copy-start.4
  0.9 0.0 copy-start.5
  0.9 0.0 copy-start.6
  0.9 0.0 copy-start.7
  0.9 1.2 %reshape.6.pairs = bf16[64,2048]{1,0:T(8,128)(2,1)S(1)} reshape(bf16[64,8,2,128]{3,2,1,0:T(2,128)(2,1)} %param.11) | data formatting | bytes 524288 | tf_op jit(solution)/shard_map/reshape | solution.py:323
  2.1 0.0 copy-done.2
  2.1 0.0 copy-done.3
  2.1 0.0 copy-done.4
  2.1 0.0 copy-done.5
  2.1 0.0 copy-done.6
  2.2 0.0 copy-done.7
  2.2 0.0 copy-start
  2.2 1.2 %copy-done = bf16[64,8192]{1,0:T(8,128)(2,1)S(1)} copy-done((bf16[64,8192]{1,0:T(8,128)(2,1)S(1)}, bf16[64,8192]{1,0:T(8,128)(2,1)}, u32[]{:S(2)}) %copy-start) | copy-done | bytes 1048600
  3.4 0.0 copy-start.1
  3.4 1.2 %copy-done.1 = bf16[256,2048]{1,0:T(8,128)(2,1)S(1)} copy-done((bf16[256,2048]{1,0:T(8,128)(2,1)S(1)}, bf16[256,2048]{1,0:T(8,128)(2,1)}, u32[]{:S(2)}) %copy-start.1) | copy-done | bytes 1048600
  4.6 43.8 %mixer.1 = bf16[64,8192]{1,0:T(8,128)(2,1)S(1)} custom-call(bf16[64,8192]{1,0:T(8,128)(2,1)S(1)} %copy-done, bf16[64,2048]{1,0:T(8,128)(2,1)S(1)} %reshape.6.pairs, bf16[256,2048]{1,0:T(8,128)(2,1)S(1)} %copy-done.1, bf16[32,256]{1,0:T(8,128)(2,1)S(1)} %bitcast.5, f32[1,32]{1,0:T(1,128)S(1)} %bitcast.7, f32[1,32]{1,0:T(1,128)S(1)} %bitcast.8, ...), custom_call_target="tpu_custom_call" | custom-call | flops 700000000 | bytes 4000000 | tf_op jit(solution)/shard_map/mixer/pallas_call | solution.py:329
  48.4 1.0 %copy.12 = bf16[64,8192]{1,0:T(8,128)(2,1)} copy(bf16[64,8192]{1,0:T(8,128)(2,1)S(1)} %mixer.1) | data formatting | bytes 2097152
Async XLA Ops:
  0.8 1.3 %copy-start.2 = (f32[5,8192]{1,0:T(8,128)S(1)}, f32[5,8192]{1,0:T(8,128)}, u32[]{:S(2)}) copy-start(f32[5,8192]{1,0:T(8,128)} %w_inner.1) | copy-start | bytes 491524
  0.8 1.3 %copy-start.3 = (bf16[256,32]{0,1:T(8,128)(2,1)S(1)}, bf16[256,32]{0,1:T(8,128)(2,1)}, u32[]{:S(2)}) copy-start(bf16[256,32]{0,1:T(8,128)(2,1)} %param.13) | copy-start | bytes 49156
  0.8 1.3 %copy-start.4 = (f32[2048]{0:T(1024)S(1)}, f32[2048]{0:T(1024)}, u32[]{:S(2)}) copy-start(f32[2048]{0:T(1024)} %param.19) | copy-start | bytes 24580
  0.9 1.3 %copy-start.5 = (f32[32]{0:T(128)S(1)}, f32[32]{0:T(128)}, u32[]{:S(2)}) copy-start(f32[32]{0:T(128)} %param.14) | copy-start | bytes 388
  0.9 1.3 %copy-start.6 = (f32[32]{0:T(128)S(1)}, f32[32]{0:T(128)}, u32[]{:S(2)}) copy-start(f32[32]{0:T(128)} %param.15) | copy-start | bytes 388
  0.9 1.3 %copy-start.7 = (f32[32]{0:T(128)S(1)}, f32[32]{0:T(128)}, u32[]{:S(2)}) copy-start(f32[32]{0:T(128)} %param.16) | copy-start | bytes 388
  2.2 1.2 %copy-start = (bf16[64,8192]{1,0:T(8,128)(2,1)S(1)}, bf16[64,8192]{1,0:T(8,128)(2,1)}, u32[]{:S(2)}) copy-start(bf16[64,8192]{1,0:T(8,128)(2,1)} %inner.1) | copy-start | bytes 3145732
  3.4 1.2 %copy-start.1 = (bf16[256,2048]{1,0:T(8,128)(2,1)S(1)}, bf16[256,2048]{1,0:T(8,128)(2,1)}, u32[]{:S(2)}) copy-start(bf16[256,2048]{1,0:T(8,128)(2,1)} %gate_hbm.1) | copy-start | bytes 3145732

commit v3 on v2

--- a/solution.py
+++ b/solution.py
@@ -11,43 +11,40 @@
 PAD = 16
 CHUNK = 32
 WIDE = 256
+LOG2E = 1.4426950408889634
 PIECE = 512
 BF = jnp.bfloat16
 F32 = jnp.float32
 
 
 def silu(v):
-    return v / (1.0 + jnp.exp(-v))
-
-
-def conv_rows(src, dst, weight, first_col, cols, dst_of):
+    half = 0.5 * v
+    return half + half * jnp.tanh(half)
+
+
+def conv_rows(src, dst, weight_of, taps, cols, wide):
     rows = src.shape[0] - PAD
-    taps = weight.shape[0] - 1
 
     def step(i, carry):
         r0 = pl.multiple_of(i * CHUNK, CHUNK)
-        for c0 in range(0, cols, WIDE):
-            raw = src[pl.ds(r0, CHUNK + PAD), c0 : c0 + WIDE].astype(F32)
-            w = weight[:, pl.ds(pl.multiple_of(first_col + c0, WIDE), WIDE)]
-            total = w[taps : taps + 1]
+        for c0 in range(0, cols, wide):
+            raw = src[pl.ds(r0, CHUNK + PAD), c0 : c0 + wide].astype(F32)
+            w = weight_of(c0)
+            total = w[taps]
             for k in range(taps):
                 o = PAD - taps + k
-                total = total + w[k : k + 1] * raw[o : o + CHUNK]
-            dst_of(dst, r0, c0, silu(total).astype(BF))
+                total = total + w[k] * raw[o : o + CHUNK]
+            dst[pl.ds(r0, CHUNK), c0 : c0 + wide] = silu(total).astype(BF)
         return carry
 
     lax.fori_loop(0, rows // CHUNK, step, 0)
-
-
-def store_plain(dst, r0, c0, value):
-    dst[pl.ds(r0, CHUNK), c0 : c0 + WIDE] = value
 
 
 def kernel(
     n, nctx, groups, heads_local,
     inner, pairs, gate_hbm, step_raw, step_bias, rate_log, skip_gain, w_inner, w_pairs, norm_gain,
     out,
-    gbuf, xraw, praw, xc, pc, mixed, ex, local, scores, cin, cout, outbuf,
+    gbuf, act, xraw, praw, xc, pc, mixed, ex, local, scores, cin, cout, outbuf,
     xs, xr, ps, pr, lsem, hs, hr, cs, cr, os, orr, olsem, gsem,
 ):
     me = lax.axis_index("head")
@@ -152,6 +149,9 @@
     tail = jnp.exp(lc[BLOCK - 1 : BLOCK, :] - shifted)
     grow = jnp.exp(lc)
 
+    lc2 = lc * LOG2E
+    shifted2_t = shifted_t * LOG2E
+
     def spread(cols, a):
         left = lax.broadcasted_iota(jnp.int32, (cols.shape[0], 2 * hd), 1) < hd
         return jnp.where(left, cols[:, a : a + 1], cols[:, a + 1 : a + 2])
@@ -173,8 +173,30 @@
         for a in range(0, per, 2):
             ex[g, :, a * hd : (a + 2) * hd] = spread(grow, g * per + a)
 
+    gate_copy.wait()
+
+    def open_gate(i, carry):
+        at = pl.ds(pl.multiple_of(i * CHUNK, CHUNK), CHUNK)
+        for c0 in range(0, width, WIDE):
+            act[at, c0 : c0 + WIDE] = silu(gate[at, c0 : c0 + WIDE].astype(F32))
+        return carry
+
+    lax.fori_loop(0, BLOCK // CHUNK, open_gate, 0)
     arrived(0, praw, [p_copy(k, to(k), source(k)) for k in range(1, n)], own[0])
-    conv_rows(praw, pc, w_pairs, me * pw, pw, store_plain)
+    taps = w_inner.shape[0] - 1
+
+    def pair_weight(c0):
+        g, b = divmod(c0 // st, 2)
+        return [w_pairs[k, me * groups + g, b : b + 1, :] for k in range(taps + 1)]
+
+    def inner_weight(q):
+        def rows_at(c0):
+            at = pl.ds(pl.multiple_of(me * width + q * PIECE + c0, WIDE), WIDE)
+            return [w_inner[k : k + 1, at] for k in range(taps + 1)]
+
+        return rows_at
+
+    conv_rows(praw, pc, pair_weight, taps, pw, st)
     bts = []
     for g in range(groups):
         bt = pc[:, 2 * g * st : (2 * g + 1) * st].astype(F32).T.astype(BF)
@@ -186,7 +208,7 @@
     def prepare(q):
         arrived(1 + q, xraw.at[q],
                 [x_copy(q, k, to(k), source(k)) for k in range(1, n)], own[1 + q])
-        conv_rows(xraw.at[q], xc.at[q], w_inner, me * width + q * PIECE, PIECE, store_plain)
+        conv_rows(xraw.at[q], xc.at[q], inner_weight(q), taps, PIECE, WIDE)
         for c0 in range(0, PIECE, WIDE):
             g, first = divmod(q * PIECE + c0, gw)
             p = first // WIDE
@@ -212,12 +234,14 @@
         top, low = [], []
         for b in (a, a + 1):
             h = g * per + b
-            col = lc[:, h : h + 1]
-            row = shifted_t[h : h + 1, :]
-            w0 = scores[g, :half, :half] * jnp.exp(jnp.minimum(col[:half] - row[:, :half], 30.0))
+            col = lc2[:, h : h + 1]
+            row = shifted2_t[h : h + 1, :]
+            w0 = scores[g, :half, :half] * jnp.exp2(jnp.minimum(col[:half] - row[:, :half], 40.0))
             top.append(jnp.dot(w0.astype(BF), x[:half], preferred_element_type=F32))
-            w1 = scores[g, half:, :] * jnp.exp(jnp.minimum(col[half:] - row, 30.0))
-            low.append(jnp.dot(w1.astype(BF), x, preferred_element_type=F32))
+            w1 = scores[g, half:, :half] * jnp.exp2(col[half:] - row[:, :half])
+            w2 = scores[g, half:, half:] * jnp.exp2(jnp.minimum(col[half:] - row[:, half:], 40.0))
+            w = jnp.concatenate([w1.astype(BF), w2.astype(BF)], axis=1)
+            low.append(jnp.dot(w, x, preferred_element_type=F32))
         left = lax.broadcasted_iota(jnp.int32, (half, 2 * hd), 1) < hd
         gain = spread(skip_gain[...], g * per + a)
         xf = x.astype(F32) * gain
@@ -255,8 +279,8 @@
             ssq = jnp.zeros((rows, 1), F32)
             for p in range(pieces):
                 cols = slice(p * WIDE, (p + 1) * WIDE)
-                z = gate[rs, g * gw + p * WIDE : g * gw + (p + 1) * WIDE].astype(F32)
-                gated = mixed[g, rs, cols] * silu(z)
+                z = act[rs, g * gw + p * WIDE : g * gw + (p + 1) * WIDE]
+                gated = mixed[g, rs, cols] * z
                 mixed[g, rs, cols] = gated
                 ssq = ssq + jnp.sum(gated * gated, axis=1, keepdims=True)
             inv = lax.rsqrt(ssq / gw + 1e-05)
@@ -273,17 +297,31 @@
                 c.start()
                 own_out.append(c)
 
-    for q in range(count):
-        prepare(q)
-        for c0 in range(q * PIECE, (q + 1) * PIECE, WIDE):
-            g, first = divmod(c0, gw)
+    def pieces_of(q):
+        return [divmod(c0, gw) for c0 in range(q * PIECE, (q + 1) * PIECE, WIDE)]
+
+    def intra_piece(q):
+        for g, first in pieces_of(q):
             for a in range(first // hd, (first + WIDE) // hd, 2):
                 intra(g, a)
+
+    def forward_piece(q):
+        for g, first in pieces_of(q):
             forward(g, first // WIDE)
-    gate_copy.wait()
-    for g in range(groups):
-        absorb(g)
-        finish(g)
+
+    prepare(0)
+    intra_piece(0)
+    for q in range(1, count):
+        prepare(q)
+        forward_piece(q - 1)
+    per_group = gw // PIECE
+    for q in range(1, count):
+        intra_piece(q)
+        if q == 1:
+            forward_piece(count - 1)
+        if q % per_group == per_group - 1:
+            absorb(q // per_group)
+            finish(q // per_group)
 
     for k in range(1, n):
         p_copy(k, to(k), me).wait_send()
@@ -321,7 +359,6 @@
     pieces = gw // WIDE
     count = width // PIECE
     pairs = pairs_raw.reshape(rows, -1)
-    w_pairs = conv_pairs.reshape(conv_pairs.shape[0], -1)
     vm = pl.BlockSpec(memory_space=pltpu.VMEM)
     hbm = pl.BlockSpec(memory_space=pl.ANY)
     far = pl.BlockSpec(memory_space=pltpu.MemorySpace.HBM)
@@ -333,6 +370,7 @@
         out_specs=hbm,
         scratch_shapes=[
             pltpu.VMEM((BLOCK, width), BF),
+            pltpu.VMEM((BLOCK, width), F32),
             pltpu.VMEM((count, PAD + BLOCK, PIECE), BF),
             pltpu.VMEM((PAD + BLOCK, pw), BF),
             pltpu.VMEM((count, BLOCK, PIECE), BF),
@@ -354,13 +392,13 @@
             dma,
         ],
         compiler_params=pltpu.CompilerParams(
-            collective_id=0, has_side_effects=True, vmem_limit_bytes=40 * 1024 * 1024),
+            collective_id=0, has_side_effects=True, vmem_limit_bytes=58 * 1024 * 1024),
         cost_estimate=pl.CostEstimate(
             flops=700_000_000, bytes_accessed=4_000_000, transcendentals=4_000_000),
         name="mixer",
     )(
         inner_raw, pairs, gate_raw, step_raw.T, step_bias[None, :], rate_log[None, :],
-        skip_gain[None, :], conv_inner, w_pairs, norm_gain[None, :],
+        skip_gain[None, :], conv_inner, conv_pairs, norm_gain[None, :],
     )
 
 

time: 49.7 us -> 49 us (0.986)
  local copies, waits for them, and re-layouts: 5.48 us -> 4.1 us
    unnamed x17 -> x1, local copies, waits for them, and re-layouts: 3.45 us -> 2.26 us
    reshape x1 -> x0, local copies, waits for them, and re-layouts: 0.81 us -> none  [on_device(): w_pairs = conv_pairs.reshape(conv_pairs.shape[0], -1)]
    reshape x1, local copies, waits for them, and re-layouts: 1.22 us -> 1.83 us  [on_device(): pairs = pairs_raw.reshape(rows, -1)]
where the time goes in v3:
time: 49 us; the launch traced here: 48.2 us
  Pallas kernels  44.1 us (90%)
  local copies, waits for them, and re-layouts  4.1 us (8%)
    pallas_call x1, Pallas kernels, on_device(): pl.pallas_call(functools.partial(kernel, n, nctx, groups, heads), out_sha...  44.1 us
    unnamed x1, local copies, waits for them, and re-layouts  2.26 us
    reshape x1, local copies, waits for them, and re-layouts, on_device(): pairs = pairs_raw.reshape(rows, -1)  1.83 us

profile of v3, /device:TPU:26, one launch (start us, length us, event | category | flops | bytes accessed | tf_op | source)
XLA Modules:
  0.0 48.2 jit_solution(435287081007422109)
XLA Ops:
  0.0 1.8 %reshape.3.pairs = bf16[64,2048]{1,0:T(8,128)(2,1)} reshape(bf16[64,8,2,128]{3,2,1,0:T(2,128)(2,1)} %param.11) | data formatting | bytes 524288 | tf_op jit(solution)/shard_map/reshape | solution.py:361
  1.8 44.1 %mixer.1 = bf16[64,8192]{1,0:T(8,128)(2,1)} custom-call(bf16[64,8192]{1,0:T(8,128)(2,1)} %inner.1, bf16[64,2048]{1,0:T(8,128)(2,1)} %reshape.3.pairs, bf16[256,2048]{1,0:T(8,128)(2,1)} %gate_hbm.1, bf16[32,256]{1,0:T(8,128)(2,1)} %bitcast.5, f32[1,32]{1,0:T(1,128)} %bitcast.7, f32[1,32]{1,0:T(1,128)} %bitcast.8, f32[1,32]{1,0:T(1,128)} %bitcast.9, ...), custom_call_target="tpu_custom_call" | custom-call | flops 700000000 | bytes 4000000 | tf_op jit(solution)/shard_map/mixer/pallas_call | solution.py:366
  46.0 2.3 %copy.12 = bf16[64,8192]{1,0:T(8,128)(2,1)} copy(bf16[64,8192]{1,0:T(8,128)(2,1)} %mixer.1) | data formatting | bytes 2097152

commit v4 on v3

--- a/solution.py
+++ b/solution.py
@@ -13,6 +13,7 @@
 WIDE = 256
 LOG2E = 1.4426950408889634
 PIECE = 512
+HOP = 128
 BF = jnp.bfloat16
 F32 = jnp.float32
 
@@ -58,6 +59,7 @@
     pw = praw.shape[1]
     st = pw // (2 * groups)
     pieces = gw // WIDE
+    hops = WIDE // HOP
     count = width // PIECE
 
     gate_copy = pltpu.make_async_copy(gate_hbm, gbuf, gsem)
@@ -117,9 +119,12 @@
 
     for k in range(1, n):
         p_copy(k, to(k), me).start()
-    for q in range(count):
-        for k in range(1, n):
-            x_copy(q, k, to(k), me).start()
+    def send_x(q):
+        if q < count:
+            for k in range(1, n):
+                x_copy(q, k, to(k), me).start()
+
+    send_x(0)
     own_rows = pl.ds(pl.multiple_of(PAD + me * rows, 16), rows)
     own = [pltpu.make_async_copy(
         pairs.at[:, pl.ds(pl.multiple_of(me * pw, 128), pw)], praw.at[own_rows, :], lsem.at[0])]
@@ -159,6 +164,7 @@
     def arrived(i, ref, waits, own_copy):
         for w in waits:
             w.wait_recv()
+        send_x(i + 1)
         own_copy.wait()
 
         @pl.when(ctx < nctx - 1)
@@ -222,9 +228,10 @@
 
             @pl.when(ctx == 0)
             def _():
-                cout[g, p] = state.astype(BF)
-                if nctx > 1:
-                    chain(g, p).start()
+                for j in range(hops):
+                    cout[g, p * hops + j] = state[:, j * HOP : (j + 1) * HOP].astype(BF)
+                    if nctx > 1:
+                        chain(g, p * hops + j).start()
 
     half = BLOCK // 2
 
@@ -251,10 +258,13 @@
     def forward(g, p):
         @pl.when(jnp.logical_and(ctx > 0, ctx < nctx - 1))
         def _():
-            chain(g, p).wait_recv()
-            decay = ex[g, BLOCK - 1 : BLOCK, p * WIDE : (p + 1) * WIDE]
-            cout[g, p] = (decay * cin[g, p].astype(F32) + local[g, p]).astype(BF)
-            chain(g, p).start()
+            for j in range(hops):
+                c = p * hops + j
+                chain(g, c).wait_recv()
+                decay = ex[g, BLOCK - 1 : BLOCK, c * HOP : (c + 1) * HOP]
+                own_state = local[g, p, :, j * HOP : (j + 1) * HOP]
+                cout[g, c] = (decay * cin[g, c].astype(F32) + own_state).astype(BF)
+                chain(g, c).start()
 
     def absorb(g):
         @pl.when(ctx > 0)
@@ -264,10 +274,12 @@
 
                 @pl.when(ctx == nctx - 1)
                 def _():
-                    chain(g, p).wait_recv()
+                    for j in range(hops):
+                        chain(g, p * hops + j).wait_recv()
 
                 cmat = pc[:, (2 * g + 1) * st : (2 * g + 2) * st]
-                carried = jnp.dot(cmat, cin[g, p], preferred_element_type=F32)
+                held = jnp.concatenate([cin[g, p * hops + j] for j in range(hops)], axis=1)
+                carried = jnp.dot(cmat, held, preferred_element_type=F32)
                 mixed[g, :, cols] = mixed[g, :, cols] + carried * ex[g, :, cols]
 
     own_out = []
@@ -339,8 +351,8 @@
         for q in range(count):
             halo(1 + q, xraw.at[q]).wait_send()
         for g in range(groups):
-            for p in range(pieces):
-                chain(g, p).wait_send()
+            for c in range(pieces * hops):
+                chain(g, c).wait_send()
 
 
 def on_device(
@@ -379,14 +391,14 @@
             pltpu.VMEM((groups, BLOCK, gw), F32),
             pltpu.VMEM((groups, pieces, st, WIDE), F32),
             pltpu.VMEM((groups, BLOCK, BLOCK), F32),
-            pltpu.VMEM((groups, pieces, st, WIDE), BF),
-            pltpu.VMEM((groups, pieces, st, WIDE), BF),
+            pltpu.VMEM((groups, gw // HOP, st, HOP), BF),
+            pltpu.VMEM((groups, gw // HOP, st, HOP), BF),
             pltpu.VMEM((groups, BLOCK, gw), BF),
             dma((count, n - 1)), dma((count, n - 1)),
             dma((n - 1,)), dma((n - 1,)),
             dma((1 + count,)),
             dma((1 + count,)), dma((1 + count,)),
-            dma((groups, pieces)), dma((groups, pieces)),
+            dma((groups, gw // HOP)), dma((groups, gw // HOP)),
             dma((groups, n - 1)), dma((groups, n - 1)),
             dma((groups,)),
             dma,

time: 49 us -> 49.4 us (level)
  the two profiles are of different devices: /device:TPU:26 before, /device:TPU:18 now
where the time goes in v4:
time: 49.4 us; the launch traced here: 49.2 us
  Pallas kernels  45.1 us (91%)
  local copies, waits for them, and re-layouts  4.1 us (8%)
    pallas_call x1, Pallas kernels, on_device(): pl.pallas_call(functools.partial(kernel, n, nctx, groups, heads), out_sha...  45.1 us
    unnamed x1, local copies, waits for them, and re-layouts  2.26 us
    reshape x1, local copies, waits for them, and re-layouts, on_device(): pairs = pairs_raw.reshape(rows, -1)  1.83 us

profile of v4, /device:TPU:18, one launch (start us, length us, event | category | flops | bytes accessed | tf_op | source)
XLA Modules:
  0.0 49.2 jit_solution(11879164446541674861)
XLA Ops:
  0.0 1.8 %reshape.3.pairs = bf16[64,2048]{1,0:T(8,128)(2,1)} reshape(bf16[64,8,2,128]{3,2,1,0:T(2,128)(2,1)} %param.11) | data formatting | bytes 524288 | tf_op jit(solution)/shard_map/reshape | solution.py:373
  1.8 45.1 %mixer.1 = bf16[64,8192]{1,0:T(8,128)(2,1)} custom-call(bf16[64,8192]{1,0:T(8,128)(2,1)} %inner.1, bf16[64,2048]{1,0:T(8,128)(2,1)} %reshape.3.pairs, bf16[256,2048]{1,0:T(8,128)(2,1)} %gate_hbm.1, bf16[32,256]{1,0:T(8,128)(2,1)} %bitcast.5, f32[1,32]{1,0:T(1,128)} %bitcast.7, f32[1,32]{1,0:T(1,128)} %bitcast.8, f32[1,32]{1,0:T(1,128)} %bitcast.9, ...), custom_call_target="tpu_custom_call" | custom-call | flops 700000000 | bytes 4000000 | tf_op jit(solution)/shard_map/mixer/pallas_call | solution.py:378
  46.9 2.3 %copy.12 = bf16[64,8192]{1,0:T(8,128)(2,1)} copy(bf16[64,8192]{1,0:T(8,128)(2,1)} %mixer.1) | data formatting | bytes 2097152

commit v5 on v4

--- a/solution.py
+++ b/solution.py
@@ -255,8 +255,8 @@
         mixed[g, :half, a * hd : (a + 2) * hd] = jnp.where(left, top[0], top[1]) + xf[:half]
         mixed[g, half:, a * hd : (a + 2) * hd] = jnp.where(left, low[0], low[1]) + xf[half:]
 
-    def forward(g, p):
-        @pl.when(jnp.logical_and(ctx > 0, ctx < nctx - 1))
+    def forward(g, p, chosen):
+        @pl.when(jnp.logical_and(chosen, ctx < nctx - 1))
         def _():
             for j in range(hops):
                 c = p * hops + j
@@ -317,23 +317,30 @@
             for a in range(first // hd, (first + WIDE) // hd, 2):
                 intra(g, a)
 
-    def forward_piece(q):
+    def forward_piece(q, chosen):
         for g, first in pieces_of(q):
-            forward(g, first // WIDE)
+            forward(g, first // WIDE, chosen)
+
+    near, far = ctx == 1, ctx > 1
 
     prepare(0)
     intra_piece(0)
     for q in range(1, count):
         prepare(q)
-        forward_piece(q - 1)
+        forward_piece(q - 1, near)
+        if q > 1:
+            forward_piece(q - 2, far)
     per_group = gw // PIECE
     for q in range(1, count):
         intra_piece(q)
         if q == 1:
-            forward_piece(count - 1)
+            forward_piece(count - 1, near)
+            forward_piece(count - 2, far)
         if q % per_group == per_group - 1:
             absorb(q // per_group)
             finish(q // per_group)
+        if q == 1:
+            forward_piece(count - 1, far)
 
     for k in range(1, n):
         p_copy(k, to(k), me).wait_send()

time: 49.4 us -> 50 us (1.012)
  the two profiles are of different devices: /device:TPU:18 before, /device:TPU:26 now
where the time goes in v5:
time: 50 us; the launch traced here: 49.8 us
  Pallas kernels  45.7 us (91%)
  local copies, waits for them, and re-layouts  4.1 us (8%)
    pallas_call x1, Pallas kernels, on_device(): pl.pallas_call(functools.partial(kernel, n, nctx, groups, heads), out_sha...  45.7 us
    unnamed x1, local copies, waits for them, and re-layouts  2.26 us
    reshape x1, local copies, waits for them, and re-layouts, on_device(): pairs = pairs_raw.reshape(rows, -1)  1.83 us

profile of v5, /device:TPU:26, one launch (start us, length us, event | category | flops | bytes accessed | tf_op | source)
XLA Modules:
  0.0 49.8 jit_solution(15529746526694548246)
XLA Ops:
  0.0 1.8 %reshape.3.pairs = bf16[64,2048]{1,0:T(8,128)(2,1)} reshape(bf16[64,8,2,128]{3,2,1,0:T(2,128)(2,1)} %param.11) | data formatting | bytes 524288 | tf_op jit(solution)/shard_map/reshape | solution.py:380
  1.8 45.7 %mixer.1 = bf16[64,8192]{1,0:T(8,128)(2,1)} custom-call(bf16[64,8192]{1,0:T(8,128)(2,1)} %inner.1, bf16[64,2048]{1,0:T(8,128)(2,1)} %reshape.3.pairs, bf16[256,2048]{1,0:T(8,128)(2,1)} %gate_hbm.1, bf16[32,256]{1,0:T(8,128)(2,1)} %bitcast.5, f32[1,32]{1,0:T(1,128)} %bitcast.7, f32[1,32]{1,0:T(1,128)} %bitcast.8, f32[1,32]{1,0:T(1,128)} %bitcast.9, ...), custom_call_target="tpu_custom_call" | custom-call | flops 700000000 | bytes 4000000 | tf_op jit(solution)/shard_map/mixer/pallas_call | solution.py:385
  47.6 2.3 %copy.12 = bf16[64,8192]{1,0:T(8,128)(2,1)} copy(bf16[64,8192]{1,0:T(8,128)(2,1)} %mixer.1) | data formatting | bytes 2097152

commit v6 on v1

--- a/solution.py
+++ b/solution.py
@@ -16,7 +16,8 @@
 
 
 def silu(v):
-    return v / (1.0 + jnp.exp(-v))
+    half = 0.5 * v
+    return half + half * jnp.tanh(half)
 
 
 def conv_rows(src, dst, weight, first_col, cols, dst_of):
@@ -44,10 +45,10 @@
 
 def kernel(
     n, nctx, groups, heads_local,
-    inner, pairs, gate, step_raw, step_bias, rate_log, skip_gain, w_inner, w_pairs, norm_gain,
+    inner, pairs, gate_hbm, step_raw, step_bias, rate_log, skip_gain, w_inner, w_pairs, norm_gain,
     out,
-    xraw, praw, xc, pc, mixed, ex, local, scores, cin, cout, outbuf,
-    xs, xr, ps, pr, lsem, hs, hr, cs, cr, os, orr, olsem,
+    gate, xraw, praw, xc, pc, mixed, ex, local, scores, cin, cout, outbuf,
+    xs, xr, ps, pr, lsem, hs, hr, cs, cr, os, orr, olsem, gsem,
 ):
     me = lax.axis_index("head")
     ctx = lax.axis_index("context")
@@ -59,6 +60,9 @@
     pw = praw.shape[1]
     st = pw // (2 * groups)
     pieces = gw // WIDE
+
+    gate_copy = pltpu.make_async_copy(gate_hbm, gate, gsem)
+    gate_copy.start()
 
     barrier = pltpu.get_barrier_semaphore()
     for k in range(1, n):
@@ -133,15 +137,16 @@
         for g in range(groups):
             xraw[g, 0:PAD, :] = jnp.zeros((PAD, gw), BF)
 
-    v = step_raw[...].astype(F32) + step_bias[...]
+    v = step_raw[...].astype(F32) + step_bias[...].T
     step = jnp.maximum(v, 0.0) + jnp.log1p(jnp.exp(-jnp.abs(v)))
     tri_r = lax.broadcasted_iota(jnp.int32, (BLOCK, BLOCK), 0)
     tri_c = lax.broadcasted_iota(jnp.int32, (BLOCK, BLOCK), 1)
     lower = tri_r >= tri_c
-    lc = jnp.dot(lower.astype(F32), -jnp.exp(rate_log[...]) * step,
-                 precision=lax.Precision.HIGHEST, preferred_element_type=F32)
-    shifted = lc - jnp.log(step)
-    shifted_t = shifted.T
+    lc_t = jnp.dot(-jnp.exp(rate_log[...].T) * step, (tri_r <= tri_c).astype(F32),
+                   precision=lax.Precision.HIGHEST, preferred_element_type=F32)
+    shifted_t = lc_t - jnp.log(step)
+    lc = lc_t.T
+    shifted = shifted_t.T
     tail = jnp.exp(lc[BLOCK - 1 : BLOCK, :] - shifted)
     grow = jnp.exp(lc)
 
@@ -264,6 +269,7 @@
                 c.start()
                 own_out.append(c)
 
+    gate_copy.wait()
     prepare(0)
     work(0)
     for g in range(1, groups):
@@ -312,9 +318,10 @@
     return pl.pallas_call(
         functools.partial(kernel, n, nctx, groups, heads),
         out_shape=jax.ShapeDtypeStruct((rows, full), BF),
-        in_specs=[hbm, hbm] + [vm] * 8,
+        in_specs=[hbm, hbm, hbm] + [vm] * 7,
         out_specs=hbm,
         scratch_shapes=[
+            pltpu.VMEM((BLOCK, width), BF),
             pltpu.VMEM((groups, PAD + BLOCK, gw), BF),
             pltpu.VMEM((PAD + BLOCK, pw), BF),
             pltpu.VMEM((groups, BLOCK, gw), BF),
@@ -333,14 +340,15 @@
             dma((groups, pieces)), dma((groups, pieces)),
             dma((groups, n - 1)), dma((groups, n - 1)),
             dma((groups,)),
+            dma,
         ],
         compiler_params=pltpu.CompilerParams(
-            collective_id=0, has_side_effects=True, vmem_limit_bytes=40 * 1024 * 1024),
+            collective_id=0, has_side_effects=True, vmem_limit_bytes=58 * 1024 * 1024),
         cost_estimate=pl.CostEstimate(
             flops=700_000_000, bytes_accessed=4_000_000, transcendentals=4_000_000),
         name="mixer",
     )(
-        inner_raw, pairs, gate_raw, step_raw, step_bias[None, :], rate_log[None, :],
+        inner_raw, pairs, gate_raw, step_raw.T, step_bias[None, :], rate_log[None, :],
         skip_gain[None, :], conv_inner, w_pairs, norm_gain[None, :],
     )
 

time: 48.5 us -> 49.7 us (1.025)
  Pallas kernels: 42.6 us -> 43.9 us
    unnamed x18 -> x1, local copies, waits for them, and re-layouts: 4.29 us -> 2.26 us
    reshape x1, local copies, waits for them, and re-layouts: 0.03 us -> 1.43 us  [on_device(): w_pairs = conv_pairs.reshape(conv_pairs.shape[0], -1)]
    pallas_call x1, Pallas kernels: 42.6 us -> 43.9 us  [on_device(): pl.pallas_call(functools.partial(kernel, n, nctx, groups, heads), out_sha...]
    reshape x1, local copies, waits for them, and re-layouts: 1.22 us -> 1.83 us  [on_device(): pairs = pairs_raw.reshape(rows, -1)]
where the time goes in v6:
time: 49.7 us; the launch traced here: 49.4 us
  Pallas kernels  43.9 us (88%)
  local copies, waits for them, and re-layouts  5.52 us (11%)
    pallas_call x1, Pallas kernels, on_device(): pl.pallas_call(functools.partial(kernel, n, nctx, groups, heads), out_sha...  43.9 us
    unnamed x1, local copies, waits for them, and re-layouts  2.26 us
    reshape x1, local copies, waits for them, and re-layouts, on_device(): pairs = pairs_raw.reshape(rows, -1)  1.83 us
    reshape x1, local copies, waits for them, and re-layouts, on_device(): w_pairs = conv_pairs.reshape(conv_pairs.shape[0], -1)  1.43 us

profile of v6, /device:TPU:26, one launch (start us, length us, event | category | flops | bytes accessed | tf_op | source)
XLA Modules:
  0.0 49.4 jit_solution(17620300847233785024)
XLA Ops:
  0.0 1.4 %reshape.7.w_pairs = f32[5,2048]{1,0:T(8,128)} reshape(f32[5,8,2,128]{3,2,1,0:T(2,128)} %param.18) | data formatting | bytes 81920 | tf_op jit(solution)/shard_map/reshape | solution.py:314
  1.4 1.8 %reshape.6.pairs = bf16[64,2048]{1,0:T(8,128)(2,1)} reshape(bf16[64,8,2,128]{3,2,1,0:T(2,128)(2,1)} %param.11) | data formatting | bytes 524288 | tf_op jit(solution)/shard_map/reshape | solution.py:313
  3.3 43.9 %mixer.1 = bf16[64,8192]{1,0:T(8,128)(2,1)} custom-call(bf16[64,8192]{1,0:T(8,128)(2,1)} %inner.1, bf16[64,2048]{1,0:T(8,128)(2,1)} %reshape.6.pairs, bf16[256,2048]{1,0:T(8,128)(2,1)} %gate_hbm.1, bf16[32,256]{1,0:T(8,128)(2,1)} %bitcast.5, f32[1,32]{1,0:T(1,128)} %bitcast.7, f32[1,32]{1,0:T(1,128)} %bitcast.8, f32[1,32]{1,0:T(1,128)} %bitcast.9, ...), custom_call_target="tpu_custom_call" | custom-call | flops 700000000 | bytes 4000000 | tf_op jit(solution)/shard_map/mixer/pallas_call | solution.py:318
  47.1 2.3 %copy.12 = bf16[64,8192]{1,0:T(8,128)(2,1)} copy(bf16[64,8192]{1,0:T(8,128)(2,1)} %mixer.1) | data formatting | bytes 2097152
